TPU v7x, 32 devices: a whole 2x2x4 slice. The times are simulated.
32 devices in a mesh: fde: 8 (over z, x), pas: 4 (over y, core).
Axes of the slice: x: 2, y: 2, z: 4, core: 2. Of those that a mesh axis runs over, the one named last changes fastest.
Arguments:
- query_fixed_encoding: bfloat16 [128, 10240], P(None, 'fde'), may hold values from -6 to 6
- passage_fde: bfloat16 [1024, 10240], P('pas', 'fde'), may hold values from -0.0625 to 0.0625
- query_tokens: bfloat16 [128, 32, 128], P('fde'), may hold values from -6 to 6
- query_token_totals: int32 [128], P('fde'), may hold values from 1 to 32
- passage_tokens: bfloat16 [1024, 256, 128], P(('fde', 'pas')), may hold values from -0.5 to 0.5
- passage_lengths: int32 [1024], P(('fde', 'pas')), may hold values from 1 to 256
- candidates: int32 [128, 128], P('fde', 'pas'), may hold values from 0 to 1023, as said below
Outputs:
- fde_scores: float32 [128, 1024], P('fde', 'pas')
- rerank: float32 [128, 128], P('fde', 'pas')
Inputs may be any that keep to these rules, and one draw needn't show every extreme that they name: Passage p is held by the device of linear index p // 32 over fde then pas. Among the 16 x 32 candidates held by one device, one quarter of the 32 devices (the same quarter for every device) is named exactly 48 times each, another quarter 2 times each, the rest not at all; within an owner device the ids are uniform and may repeat.
All inputs are finite; a program needn't handle non-finite values.
Results may differ from a plain program's by a relative error of at most 0.0003.
Values may be sent and summed in bfloat16 or wider, within the bound.
A program may use at most 128 MiB of HBM per device.

v0:
```python
import jax
import jax.numpy as jnp
from jax import lax
from jax.sharding import PartitionSpec as P

slot_block = 128


def maxsim_block(token_vectors, counts, local_ids, passage_tokens, passage_lengths):
    corpus_texts = jnp.take(passage_tokens, local_ids, axis=0)
    lengths = jnp.take(passage_lengths, local_ids, axis=0)
    similarity_matrix = jnp.einsum(
        "zxg,zwg->zxw", token_vectors, corpus_texts, preferred_element_type=jnp.float32
    )
    positions = lax.broadcasted_iota(jnp.int32, similarity_matrix.shape, 2)
    best_match = jnp.max(
        jnp.where(positions < lengths[:, None, None], similarity_matrix, jnp.float32(-1e30)), axis=2
    )
    token_slot = lax.broadcasted_iota(jnp.int32, best_match.shape, 1)
    summed = jnp.sum(jnp.where(token_slot < counts[:, None], best_match, jnp.float32(0.0)), axis=1)
    return summed / counts.astype(jnp.float32)


def body(
    query_fixed_encoding,
    passage_fde,
    query_tokens,
    query_token_totals,
    passage_tokens,
    passage_lengths,
    candidates,
):
    groups = lax.axis_size("fde")
    shards = lax.axis_size("pas")
    owners = groups * shards
    query_local = query_tokens.shape[0]
    incomplete_scores = jnp.einsum(
        "qf,pf->qp", query_fixed_encoding, passage_fde, preferred_element_type=jnp.float32
    )
    summed_scores = lax.psum(incomplete_scores, "fde")
    fde_scores = lax.dynamic_slice_in_dim(
        summed_scores, lax.axis_index("fde") * query_local, query_local, 0
    )
    pass_local = passage_tokens.shape[0]
    cand_local = candidates.shape[1]
    flat_ids = candidates.reshape(-1)
    pair_count = flat_ids.shape[0]
    capacity = 3 * pair_count // owners
    slot_count = owners * capacity
    count_per_block = slot_count // slot_block
    owner_dev = flat_ids // pass_local
    local_ids = flat_ids % pass_local
    onehot = (owner_dev[:, None] == jnp.arange(owners, dtype=jnp.int32)[None, :]).astype(jnp.int32)
    before = jnp.cumsum(onehot, axis=0) - onehot
    slot_rank = jnp.sum(before * onehot, axis=1)
    target = owner_dev * capacity + slot_rank
    pair_row = jnp.arange(pair_count, dtype=jnp.int32) // cand_local

    def shaped(array):
        return array.reshape((groups, shards, capacity) + array.shape[1:])

    def blocked(array):
        return array.reshape((count_per_block, slot_block) + array.shape[3:])

    send_local = jnp.zeros((slot_count,), jnp.int32).at[target].set(local_ids)
    all_tokens, all_counts = (
        lax.all_gather(query_tokens, "fde", axis=0, tiled=True),
        lax.all_gather(query_token_totals, "fde", axis=0, tiled=True),
    )
    query_ids = lax.axis_index("fde") * query_local + pair_row
    send_query = jnp.zeros((slot_count,), jnp.int32).at[target].set(query_ids)
    recv_query, recv_local = (
        lax.all_to_all(
            lax.all_to_all(shaped(send_query), "fde", split_axis=0, concat_axis=0, tiled=True),
            "pas",
            split_axis=1,
            concat_axis=1,
            tiled=True,
        ),
        lax.all_to_all(
            lax.all_to_all(shaped(send_local), "fde", split_axis=0, concat_axis=0, tiled=True),
            "pas",
            split_axis=1,
            concat_axis=1,
            tiled=True,
        ),
    )

    def score_gathered(inputs):
        query_block, local_block = inputs
        return maxsim_block(
            jnp.take(all_tokens, query_block, axis=0),
            jnp.take(all_counts, query_block, axis=0),
            local_block,
            passage_tokens,
            passage_lengths,
        )

    scores = lax.map(score_gathered, (blocked(recv_query), blocked(recv_local)))
    returned = lax.all_to_all(
        lax.all_to_all(shaped(scores.reshape(-1)), "fde", split_axis=0, concat_axis=0, tiled=True),
        "pas",
        split_axis=1,
        concat_axis=1,
        tiled=True,
    )
    rerank = jnp.take(returned.reshape(-1), target, axis=0).reshape(candidates.shape)
    return (fde_scores, rerank)


def solution(mesh):
    return jax.shard_map(
        body,
        mesh=mesh,
        in_specs=(
            P(None, "fde"),
            P("pas", "fde"),
            P("fde", None, None),
            P("fde"),
            P(("fde", "pas"), None, None),
            P(("fde", "pas")),
            P("fde", "pas"),
        ),
        out_specs=(P("fde", "pas"), P("fde", "pas")),
        check_vma=False,
    )
```

profile of v0, /device:TPU:0, one launch (start us, length us, event | category | flops | bytes accessed | tf_op | source)
XLA Modules:
  0.0 312.4 jit_solution(5663295558901833315)
XLA Ops:
  15.1 7.3 %all-to-all-start = ((s32[8,1,192]{2,1,0:T(1,128)}), s32[8,1,192]{2,1,0:T(1,128)S(1)}, u32[]{:S(2)}, u32[]{:S(2)}) async-start(s32[8,1,192]{2,1,0:T(1,128)} %reshape.331), calls=%async_computation | async-start | bytes 16384 | tf_op jit(solution)/shard_map/all_to_all | solution.py:74
  25.6 3.3 %all-to-all-done = s32[8,1,192]{2,1,0:T(1,128)S(1)} async-done(((s32[8,1,192]{2,1,0:T(1,128)}), s32[8,1,192]{2,1,0:T(1,128)S(1)}, u32[]{:S(2)}, u32[]{:S(2)}) %all-to-all-start) | async-done | bytes 6176 | tf_op jit(solution)/shard_map/all_to_all | solution.py:74
  28.9 3.3 %all-to-all-start.2 = ((s32[8,1,192]{2,1,0:T(1,128)}), s32[8,1,192]{2,1,0:T(1,128)S(1)}, u32[]{:S(2)}, u32[]{:S(2)}) async-start(s32[8,1,192]{2,1,0:T(1,128)} %reshape.335), calls=%async_computation.2 | async-start | bytes 16384 | tf_op jit(solution)/shard_map/all_to_all | solution.py:81
  34.3 4.4 %all-to-all-done.2 = s32[8,1,192]{2,1,0:T(1,128)S(1)} async-done(((s32[8,1,192]{2,1,0:T(1,128)}), s32[8,1,192]{2,1,0:T(1,128)S(1)}, u32[]{:S(2)}, u32[]{:S(2)}) %all-to-all-start.2) | async-done | bytes 6176 | tf_op jit(solution)/shard_map/all_to_all | solution.py:81
  53.7 8.5 %all-reduce = s32[128]{0:T(128)S(1)} all-reduce(s32[128]{0:T(128)S(1)} %dynamic-update-slice), channel_id=1, replica_groups=mesh['fde'=8,'pas'=4] {'fde'}, use_global_device_ids=true, to_apply=%add | all-reduce | flops 128 | bytes 1024
  64.1 212.7 %while.10 = (s32[]{:T(128)}, f32[12,128]{1,0:T(8,128)S(1)}, s32[12,128]{1,0:T(8,128)S(1)}, s32[128]{0:T(128)S(1)}, s32[12,128]{1,0:T(8,128)S(1)}, /*index=5*/s32...) while((s32[]{:T(128)}, f32[12,128]{1,0:T(8,128)S(1)}, ...), condition=%wide.region_9.10_spmd, body=%wide.region_6.9_spmd.sunk | while | flops 276313600 | bytes 32562324 | solution.py:99
  67.0 8.0 %gather_fusion.1 = bf16[128,256,128]{2,1,0:T(8,128)(2,1)} fusion(bf16[32,256,128]{2,1,0:T(8,128)(2,1)} %get-tuple-element.157, s32[1024]{0:T(1024)S(1)} %pad_clamp_fusion.5), kind=kCustom, calls=%fused_computation.3.clone.1 | custom fusion | bytes 16777728 | tf_op jit(solution)/shard_map/while/body/eval_jaxpr/jit(_take)/gather | solution.py:10
  75.8 5.8 %select_reduce_fusion.4 = f32[128,32]{1,0:T(8,128)S(1)} fusion(s32[128]{0:T(128)S(1)} %get-tuple-element.125, bf16[128,256,128]{2,1,0:T(8,128)(2,1)} %gather_fusion.1, pred[128]{0:T(512)(128)(4,1)S(1)} %get-tuple-element.126, bf16[128,32,128]{2,1,0:T(8,128)(2,1)S(1)} %gather_fusion.2, pred[128]{0:T(512)(128)(4,1)S(1)} %get-tuple-element.128), kind=kOutput, calls=%fused_computation.10.clone.1 | convolution fusion | flops 276295680 | bytes 9454336 | tf_op jit(solution)/shard_map/while/body/eval_jaxpr/zxg,zwg->zxw/dot_general | solution.py:12
  84.8 8.0 %gather_fusion.1 = bf16[128,256,128]{2,1,0:T(8,128)(2,1)} fusion(bf16[32,256,128]{2,1,0:T(8,128)(2,1)} %get-tuple-element.157, s32[1024]{0:T(1024)S(1)} %pad_clamp_fusion.5), kind=kCustom, calls=%fused_computation.3.clone.1 | custom fusion | bytes 16777728 | tf_op jit(solution)/shard_map/while/body/eval_jaxpr/jit(_take)/gather | solution.py:10
  93.6 5.8 %select_reduce_fusion.4 = f32[128,32]{1,0:T(8,128)S(1)} fusion(s32[128]{0:T(128)S(1)} %get-tuple-element.125, bf16[128,256,128]{2,1,0:T(8,128)(2,1)} %gather_fusion.1, pred[128]{0:T(512)(128)(4,1)S(1)} %get-tuple-element.126, bf16[128,32,128]{2,1,0:T(8,128)(2,1)S(1)} %gather_fusion.2, pred[128]{0:T(512)(128)(4,1)S(1)} %get-tuple-element.128), kind=kOutput, calls=%fused_computation.10.clone.1 | convolution fusion | flops 276295680 | bytes 9454336 | tf_op jit(solution)/shard_map/while/body/eval_jaxpr/zxg,zwg->zxw/dot_general | solution.py:12
  102.6 8.0 %gather_fusion.1 = bf16[128,256,128]{2,1,0:T(8,128)(2,1)} fusion(bf16[32,256,128]{2,1,0:T(8,128)(2,1)} %get-tuple-element.157, s32[1024]{0:T(1024)S(1)} %pad_clamp_fusion.5), kind=kCustom, calls=%fused_computation.3.clone.1 | custom fusion | bytes 16777728 | tf_op jit(solution)/shard_map/while/body/eval_jaxpr/jit(_take)/gather | solution.py:10
  111.3 5.8 %select_reduce_fusion.4 = f32[128,32]{1,0:T(8,128)S(1)} fusion(s32[128]{0:T(128)S(1)} %get-tuple-element.125, bf16[128,256,128]{2,1,0:T(8,128)(2,1)} %gather_fusion.1, pred[128]{0:T(512)(128)(4,1)S(1)} %get-tuple-element.126, bf16[128,32,128]{2,1,0:T(8,128)(2,1)S(1)} %gather_fusion.2, pred[128]{0:T(512)(128)(4,1)S(1)} %get-tuple-element.128), kind=kOutput, calls=%fused_computation.10.clone.1 | convolution fusion | flops 276295680 | bytes 9454336 | tf_op jit(solution)/shard_map/while/body/eval_jaxpr/zxg,zwg->zxw/dot_general | solution.py:12
  120.3 8.0 %gather_fusion.1 = bf16[128,256,128]{2,1,0:T(8,128)(2,1)} fusion(bf16[32,256,128]{2,1,0:T(8,128)(2,1)} %get-tuple-element.157, s32[1024]{0:T(1024)S(1)} %pad_clamp_fusion.5), kind=kCustom, calls=%fused_computation.3.clone.1 | custom fusion | bytes 16777728 | tf_op jit(solution)/shard_map/while/body/eval_jaxpr/jit(_take)/gather | solution.py:10
  129.1 5.8 %select_reduce_fusion.4 = f32[128,32]{1,0:T(8,128)S(1)} fusion(s32[128]{0:T(128)S(1)} %get-tuple-element.125, bf16[128,256,128]{2,1,0:T(8,128)(2,1)} %gather_fusion.1, pred[128]{0:T(512)(128)(4,1)S(1)} %get-tuple-element.126, bf16[128,32,128]{2,1,0:T(8,128)(2,1)S(1)} %gather_fusion.2, pred[128]{0:T(512)(128)(4,1)S(1)} %get-tuple-element.128), kind=kOutput, calls=%fused_computation.10.clone.1 | convolution fusion | flops 276295680 | bytes 9454336 | tf_op jit(solution)/shard_map/while/body/eval_jaxpr/zxg,zwg->zxw/dot_general | solution.py:12
  138.0 8.2 %gather_fusion.1 = bf16[128,256,128]{2,1,0:T(8,128)(2,1)} fusion(bf16[32,256,128]{2,1,0:T(8,128)(2,1)} %get-tuple-element.157, s32[1024]{0:T(1024)S(1)} %pad_clamp_fusion.5), kind=kCustom, calls=%fused_computation.3.clone.1 | custom fusion | bytes 16777728 | tf_op jit(solution)/shard_map/while/body/eval_jaxpr/jit(_take)/gather | solution.py:10
  147.0 5.8 %select_reduce_fusion.4 = f32[128,32]{1,0:T(8,128)S(1)} fusion(s32[128]{0:T(128)S(1)} %get-tuple-element.125, bf16[128,256,128]{2,1,0:T(8,128)(2,1)} %gather_fusion.1, pred[128]{0:T(512)(128)(4,1)S(1)} %get-tuple-element.126, bf16[128,32,128]{2,1,0:T(8,128)(2,1)S(1)} %gather_fusion.2, pred[128]{0:T(512)(128)(4,1)S(1)} %get-tuple-element.128), kind=kOutput, calls=%fused_computation.10.clone.1 | convolution fusion | flops 276295680 | bytes 9454336 | tf_op jit(solution)/shard_map/while/body/eval_jaxpr/zxg,zwg->zxw/dot_general | solution.py:12
  155.9 7.9 %gather_fusion.1 = bf16[128,256,128]{2,1,0:T(8,128)(2,1)} fusion(bf16[32,256,128]{2,1,0:T(8,128)(2,1)} %get-tuple-element.157, s32[1024]{0:T(1024)S(1)} %pad_clamp_fusion.5), kind=kCustom, calls=%fused_computation.3.clone.1 | custom fusion | bytes 16777728 | tf_op jit(solution)/shard_map/while/body/eval_jaxpr/jit(_take)/gather | solution.py:10
  164.6 5.8 %select_reduce_fusion.4 = f32[128,32]{1,0:T(8,128)S(1)} fusion(s32[128]{0:T(128)S(1)} %get-tuple-element.125, bf16[128,256,128]{2,1,0:T(8,128)(2,1)} %gather_fusion.1, pred[128]{0:T(512)(128)(4,1)S(1)} %get-tuple-element.126, bf16[128,32,128]{2,1,0:T(8,128)(2,1)S(1)} %gather_fusion.2, pred[128]{0:T(512)(128)(4,1)S(1)} %get-tuple-element.128), kind=kOutput, calls=%fused_computation.10.clone.1 | convolution fusion | flops 276295680 | bytes 9454336 | tf_op jit(solution)/shard_map/while/body/eval_jaxpr/zxg,zwg->zxw/dot_general | solution.py:12
  173.6 7.9 %gather_fusion.1 = bf16[128,256,128]{2,1,0:T(8,128)(2,1)} fusion(bf16[32,256,128]{2,1,0:T(8,128)(2,1)} %get-tuple-element.157, s32[1024]{0:T(1024)S(1)} %pad_clamp_fusion.5), kind=kCustom, calls=%fused_computation.3.clone.1 | custom fusion | bytes 16777728 | tf_op jit(solution)/shard_map/while/body/eval_jaxpr/jit(_take)/gather | solution.py:10
  182.3 5.8 %select_reduce_fusion.4 = f32[128,32]{1,0:T(8,128)S(1)} fusion(s32[128]{0:T(128)S(1)} %get-tuple-element.125, bf16[128,256,128]{2,1,0:T(8,128)(2,1)} %gather_fusion.1, pred[128]{0:T(512)(128)(4,1)S(1)} %get-tuple-element.126, bf16[128,32,128]{2,1,0:T(8,128)(2,1)S(1)} %gather_fusion.2, pred[128]{0:T(512)(128)(4,1)S(1)} %get-tuple-element.128), kind=kOutput, calls=%fused_computation.10.clone.1 | convolution fusion | flops 276295680 | bytes 9454336 | tf_op jit(solution)/shard_map/while/body/eval_jaxpr/zxg,zwg->zxw/dot_general | solution.py:12
  191.2 8.0 %gather_fusion.1 = bf16[128,256,128]{2,1,0:T(8,128)(2,1)} fusion(bf16[32,256,128]{2,1,0:T(8,128)(2,1)} %get-tuple-element.157, s32[1024]{0:T(1024)S(1)} %pad_clamp_fusion.5), kind=kCustom, calls=%fused_computation.3.clone.1 | custom fusion | bytes 16777728 | tf_op jit(solution)/shard_map/while/body/eval_jaxpr/jit(_take)/gather | solution.py:10
  200.0 5.8 %select_reduce_fusion.4 = f32[128,32]{1,0:T(8,128)S(1)} fusion(s32[128]{0:T(128)S(1)} %get-tuple-element.125, bf16[128,256,128]{2,1,0:T(8,128)(2,1)} %gather_fusion.1, pred[128]{0:T(512)(128)(4,1)S(1)} %get-tuple-element.126, bf16[128,32,128]{2,1,0:T(8,128)(2,1)S(1)} %gather_fusion.2, pred[128]{0:T(512)(128)(4,1)S(1)} %get-tuple-element.128), kind=kOutput, calls=%fused_computation.10.clone.1 | convolution fusion | flops 276295680 | bytes 9454336 | tf_op jit(solution)/shard_map/while/body/eval_jaxpr/zxg,zwg->zxw/dot_general | solution.py:12
  209.0 8.0 %gather_fusion.1 = bf16[128,256,128]{2,1,0:T(8,128)(2,1)} fusion(bf16[32,256,128]{2,1,0:T(8,128)(2,1)} %get-tuple-element.157, s32[1024]{0:T(1024)S(1)} %pad_clamp_fusion.5), kind=kCustom, calls=%fused_computation.3.clone.1 | custom fusion | bytes 16777728 | tf_op jit(solution)/shard_map/while/body/eval_jaxpr/jit(_take)/gather | solution.py:10
  217.7 5.8 %select_reduce_fusion.4 = f32[128,32]{1,0:T(8,128)S(1)} fusion(s32[128]{0:T(128)S(1)} %get-tuple-element.125, bf16[128,256,128]{2,1,0:T(8,128)(2,1)} %gather_fusion.1, pred[128]{0:T(512)(128)(4,1)S(1)} %get-tuple-element.126, bf16[128,32,128]{2,1,0:T(8,128)(2,1)S(1)} %gather_fusion.2, pred[128]{0:T(512)(128)(4,1)S(1)} %get-tuple-element.128), kind=kOutput, calls=%fused_computation.10.clone.1 | convolution fusion | flops 276295680 | bytes 9454336 | tf_op jit(solution)/shard_map/while/body/eval_jaxpr/zxg,zwg->zxw/dot_general | solution.py:12
  226.7 7.9 %gather_fusion.1 = bf16[128,256,128]{2,1,0:T(8,128)(2,1)} fusion(bf16[32,256,128]{2,1,0:T(8,128)(2,1)} %get-tuple-element.157, s32[1024]{0:T(1024)S(1)} %pad_clamp_fusion.5), kind=kCustom, calls=%fused_computation.3.clone.1 | custom fusion | bytes 16777728 | tf_op jit(solution)/shard_map/while/body/eval_jaxpr/jit(_take)/gather | solution.py:10
  235.4 5.8 %select_reduce_fusion.4 = f32[128,32]{1,0:T(8,128)S(1)} fusion(s32[128]{0:T(128)S(1)} %get-tuple-element.125, bf16[128,256,128]{2,1,0:T(8,128)(2,1)} %gather_fusion.1, pred[128]{0:T(512)(128)(4,1)S(1)} %get-tuple-element.126, bf16[128,32,128]{2,1,0:T(8,128)(2,1)S(1)} %gather_fusion.2, pred[128]{0:T(512)(128)(4,1)S(1)} %get-tuple-element.128), kind=kOutput, calls=%fused_computation.10.clone.1 | convolution fusion | flops 276295680 | bytes 9454336 | tf_op jit(solution)/shard_map/while/body/eval_jaxpr/zxg,zwg->zxw/dot_general | solution.py:12
  244.3 8.0 %gather_fusion.1 = bf16[128,256,128]{2,1,0:T(8,128)(2,1)} fusion(bf16[32,256,128]{2,1,0:T(8,128)(2,1)} %get-tuple-element.157, s32[1024]{0:T(1024)S(1)} %pad_clamp_fusion.5), kind=kCustom, calls=%fused_computation.3.clone.1 | custom fusion | bytes 16777728 | tf_op jit(solution)/shard_map/while/body/eval_jaxpr/jit(_take)/gather | solution.py:10
  253.1 5.8 %select_reduce_fusion.4 = f32[128,32]{1,0:T(8,128)S(1)} fusion(s32[128]{0:T(128)S(1)} %get-tuple-element.125, bf16[128,256,128]{2,1,0:T(8,128)(2,1)} %gather_fusion.1, pred[128]{0:T(512)(128)(4,1)S(1)} %get-tuple-element.126, bf16[128,32,128]{2,1,0:T(8,128)(2,1)S(1)} %gather_fusion.2, pred[128]{0:T(512)(128)(4,1)S(1)} %get-tuple-element.128), kind=kOutput, calls=%fused_computation.10.clone.1 | convolution fusion | flops 276295680 | bytes 9454336 | tf_op jit(solution)/shard_map/while/body/eval_jaxpr/zxg,zwg->zxw/dot_general | solution.py:12
  262.1 7.9 %gather_fusion.1 = bf16[128,256,128]{2,1,0:T(8,128)(2,1)} fusion(bf16[32,256,128]{2,1,0:T(8,128)(2,1)} %get-tuple-element.157, s32[1024]{0:T(1024)S(1)} %pad_clamp_fusion.5), kind=kCustom, calls=%fused_computation.3.clone.1 | custom fusion | bytes 16777728 | tf_op jit(solution)/shard_map/while/body/eval_jaxpr/jit(_take)/gather | solution.py:10
  270.8 5.8 %select_reduce_fusion.4 = f32[128,32]{1,0:T(8,128)S(1)} fusion(s32[128]{0:T(128)S(1)} %get-tuple-element.125, bf16[128,256,128]{2,1,0:T(8,128)(2,1)} %gather_fusion.1, pred[128]{0:T(512)(128)(4,1)S(1)} %get-tuple-element.126, bf16[128,32,128]{2,1,0:T(8,128)(2,1)S(1)} %gather_fusion.2, pred[128]{0:T(512)(128)(4,1)S(1)} %get-tuple-element.128), kind=kOutput, calls=%fused_computation.10.clone.1 | convolution fusion | flops 276295680 | bytes 9454336 | tf_op jit(solution)/shard_map/while/body/eval_jaxpr/zxg,zwg->zxw/dot_general | solution.py:12
  277.6 7.7 %all-to-all-start.4 = ((f32[8,1,192]{2,1,0:T(1,128)}), f32[8,1,192]{2,1,0:T(1,128)S(1)}, u32[]{:S(2)}, u32[]{:S(2)}) async-start(f32[8,1,192]{2,1,0:T(1,128)} %reshape.339), calls=%async_computation.4 | async-start | bytes 16384 | tf_op jit(solution)/shard_map/all_to_all | solution.py:101
  285.3 6.4 %all-to-all-done.4 = f32[8,1,192]{2,1,0:T(1,128)S(1)} async-done(((f32[8,1,192]{2,1,0:T(1,128)}), f32[8,1,192]{2,1,0:T(1,128)S(1)}, u32[]{:S(2)}, u32[]{:S(2)}) %all-to-all-start.4) | async-done | bytes 6176 | tf_op jit(solution)/shard_map/all_to_all | solution.py:101
  (230 shorter events, 90.4 us)
Async XLA Ops:
  7.2 41.9 %copy-start = (bf16[256,1280]{1,0:T(8,128)(2,1)S(1)}, bf16[256,1280]{1,0:T(8,128)(2,1)}, u32[]{:S(2)}) copy-start(bf16[256,1280]{1,0:T(8,128)(2,1)} %param.10) | copy-start | bytes 1966084
  7.2 56.9 %all-gather.2.cloned.1.call-start = ((), (), s32[]{:S(2)}) async-start(), calls=%async_computation.7 | async-start | bytes 1179648 | tf_op jit(solution)/shard_map/all_gather | solution.py:67
  15.1 13.8 %all-to-all-start = ((s32[8,1,192]{2,1,0:T(1,128)}), s32[8,1,192]{2,1,0:T(1,128)S(1)}, u32[]{:S(2)}, u32[]{:S(2)}) async-start(s32[8,1,192]{2,1,0:T(1,128)} %reshape.331), calls=%async_computation | async-start | bytes 16384 | tf_op jit(solution)/shard_map/all_to_all | solution.py:74
  28.9 9.8 %all-to-all-start.2 = ((s32[8,1,192]{2,1,0:T(1,128)}), s32[8,1,192]{2,1,0:T(1,128)S(1)}, u32[]{:S(2)}, u32[]{:S(2)}) async-start(s32[8,1,192]{2,1,0:T(1,128)} %reshape.335), calls=%async_computation.2 | async-start | bytes 16384 | tf_op jit(solution)/shard_map/all_to_all | solution.py:81
  38.7 7.0 %all-to-all-start.1 = ((s32[4,1,384]{2,1,0:T(1,128)}), s32[4,1,384]{2,1,0:T(1,128)S(1)}, u32[]{:S(2)}, u32[]{:S(2)}) async-start(s32[4,1,384]{2,1,0:T(1,128)} %reshape.333), calls=%async_computation.1 | async-start | bytes 12288 | tf_op jit(solution)/shard_map/all_to_all | solution.py:73
  45.7 17.4 %all-to-all-start.3 = ((s32[4,1,384]{2,1,0:T(1,128)}), s32[4,1,384]{2,1,0:T(1,128)S(1)}, u32[]{:S(2)}, u32[]{:S(2)}) async-start(s32[4,1,384]{2,1,0:T(1,128)} %reshape.337), calls=%async_computation.3 | async-start | bytes 12288 | tf_op jit(solution)/shard_map/all_to_all | solution.py:80
  49.0 248.1 %all-reduce.3.cloned.1.call-start = ((), (), s32[]{:S(2)}) async-start(), calls=%async_computation.6 | async-start | bytes 262144 | tf_op jit(solution)/shard_map/psum | solution.py:40
  64.1 240.9 %copy-start.2 = (s32[16,32]{1,0:T(8,128)S(1)}, s32[16,32]{1,0:T(8,128)}, u32[]{:S(2)}) copy-start(s32[16,32]{1,0:T(8,128)} %param.15) | copy-start | bytes 6148
  67.0 8.0 %copy-start.1 = (bf16[128,32,128]{2,1,0:T(8,128)(2,1)S(1)}, bf16[128,32,128]{2,1,0:T(8,128)(2,1)}, u32[]{:S(2)}) copy-start(bf16[128,32,128]{2,1,0:T(8,128)(2,1)} %get-tuple-element.156) | copy-start | bytes 3145732 | tf_op jit(solution)/shard_map/while
  84.8 8.0 %copy-start.1 = (bf16[128,32,128]{2,1,0:T(8,128)(2,1)S(1)}, bf16[128,32,128]{2,1,0:T(8,128)(2,1)}, u32[]{:S(2)}) copy-start(bf16[128,32,128]{2,1,0:T(8,128)(2,1)} %get-tuple-element.156) | copy-start | bytes 3145732 | tf_op jit(solution)/shard_map/while
  102.5 8.0 %copy-start.1 = (bf16[128,32,128]{2,1,0:T(8,128)(2,1)S(1)}, bf16[128,32,128]{2,1,0:T(8,128)(2,1)}, u32[]{:S(2)}) copy-start(bf16[128,32,128]{2,1,0:T(8,128)(2,1)} %get-tuple-element.156) | copy-start | bytes 3145732 | tf_op jit(solution)/shard_map/while
  120.3 8.0 %copy-start.1 = (bf16[128,32,128]{2,1,0:T(8,128)(2,1)S(1)}, bf16[128,32,128]{2,1,0:T(8,128)(2,1)}, u32[]{:S(2)}) copy-start(bf16[128,32,128]{2,1,0:T(8,128)(2,1)} %get-tuple-element.156) | copy-start | bytes 3145732 | tf_op jit(solution)/shard_map/while
  138.0 8.2 %copy-start.1 = (bf16[128,32,128]{2,1,0:T(8,128)(2,1)S(1)}, bf16[128,32,128]{2,1,0:T(8,128)(2,1)}, u32[]{:S(2)}) copy-start(bf16[128,32,128]{2,1,0:T(8,128)(2,1)} %get-tuple-element.156) | copy-start | bytes 3145732 | tf_op jit(solution)/shard_map/while
  155.9 7.9 %copy-start.1 = (bf16[128,32,128]{2,1,0:T(8,128)(2,1)S(1)}, bf16[128,32,128]{2,1,0:T(8,128)(2,1)}, u32[]{:S(2)}) copy-start(bf16[128,32,128]{2,1,0:T(8,128)(2,1)} %get-tuple-element.156) | copy-start | bytes 3145732 | tf_op jit(solution)/shard_map/while
  173.6 7.9 %copy-start.1 = (bf16[128,32,128]{2,1,0:T(8,128)(2,1)S(1)}, bf16[128,32,128]{2,1,0:T(8,128)(2,1)}, u32[]{:S(2)}) copy-start(bf16[128,32,128]{2,1,0:T(8,128)(2,1)} %get-tuple-element.156) | copy-start | bytes 3145732 | tf_op jit(solution)/shard_map/while
  191.2 8.0 %copy-start.1 = (bf16[128,32,128]{2,1,0:T(8,128)(2,1)S(1)}, bf16[128,32,128]{2,1,0:T(8,128)(2,1)}, u32[]{:S(2)}) copy-start(bf16[128,32,128]{2,1,0:T(8,128)(2,1)} %get-tuple-element.156) | copy-start | bytes 3145732 | tf_op jit(solution)/shard_map/while
  209.0 8.0 %copy-start.1 = (bf16[128,32,128]{2,1,0:T(8,128)(2,1)S(1)}, bf16[128,32,128]{2,1,0:T(8,128)(2,1)}, u32[]{:S(2)}) copy-start(bf16[128,32,128]{2,1,0:T(8,128)(2,1)} %get-tuple-element.156) | copy-start | bytes 3145732 | tf_op jit(solution)/shard_map/while
  226.7 7.9 %copy-start.1 = (bf16[128,32,128]{2,1,0:T(8,128)(2,1)S(1)}, bf16[128,32,128]{2,1,0:T(8,128)(2,1)}, u32[]{:S(2)}) copy-start(bf16[128,32,128]{2,1,0:T(8,128)(2,1)} %get-tuple-element.156) | copy-start | bytes 3145732 | tf_op jit(solution)/shard_map/while
  244.3 8.0 %copy-start.1 = (bf16[128,32,128]{2,1,0:T(8,128)(2,1)S(1)}, bf16[128,32,128]{2,1,0:T(8,128)(2,1)}, u32[]{:S(2)}) copy-start(bf16[128,32,128]{2,1,0:T(8,128)(2,1)} %get-tuple-element.156) | copy-start | bytes 3145732 | tf_op jit(solution)/shard_map/while
  262.1 7.9 %copy-start.1 = (bf16[128,32,128]{2,1,0:T(8,128)(2,1)S(1)}, bf16[128,32,128]{2,1,0:T(8,128)(2,1)}, u32[]{:S(2)}) copy-start(bf16[128,32,128]{2,1,0:T(8,128)(2,1)} %get-tuple-element.156) | copy-start | bytes 3145732 | tf_op jit(solution)/shard_map/while
  277.6 14.2 %all-to-all-start.4 = ((f32[8,1,192]{2,1,0:T(1,128)}), f32[8,1,192]{2,1,0:T(1,128)S(1)}, u32[]{:S(2)}, u32[]{:S(2)}) async-start(f32[8,1,192]{2,1,0:T(1,128)} %reshape.339), calls=%async_computation.4 | async-start | bytes 16384 | tf_op jit(solution)/shard_map/all_to_all | solution.py:101
  293.8 7.0 %all-to-all-start.5 = ((f32[4,1,384]{2,1,0:T(1,128)}), f32[4,1,384]{2,1,0:T(1,128)S(1)}, u32[]{:S(2)}, u32[]{:S(2)}) async-start(f32[4,1,384]{2,1,0:T(1,128)} %reshape.341), calls=%async_computation.5 | async-start | bytes 12288 | tf_op jit(solution)/shard_map/all_to_all | solution.py:100
Sparse Core Ops, SparseCore 0:
  10.1 42.7 all-gather.1
  56.3 68.4 all-reduce.2
where the time goes:
time: 313 us; the launch traced here: 312 us
  local copies, waits for them, and re-layouts  160 us (51%)
  matrix products  71.4 us (23%)
  starting transfers between devices  28.1 us (9%)
  waiting for transfers between devices  19.6 us (6%)
  between operations  14.8 us (5%)
  other arithmetic  9.27 us (3%)
  blocking collectives  8.54 us (3%)
    gather x12, local copies, waits for them, and re-layouts, maxsim_block(): corpus_texts = jnp.take(passage_tokens, local_ids, axis=0)  95.8 us
    dot_general x12, matrix products, maxsim_block(): jnp.einsum('zxg,zwg->zxw', token_vectors, corpus_texts, preferred_element...  69.4 us
    gather x12, local copies, waits for them, and re-layouts, maxsim_block(): lengths = jnp.take(passage_lengths, local_ids, axis=0)  19 us
    gather x12, local copies, waits for them, and re-layouts, score_gathered(): jnp.take(all_counts, query_block, axis=0)  14.7 us
    gather x12, local copies, waits for them, and re-layouts, score_gathered(): jnp.take(all_tokens, query_block, axis=0)  9.18 us
    unnamed x1, blocking collectives  8.54 us
    all_to_all x1, starting transfers between devices, body(): lax.all_to_all(shaped(scores.reshape(-1)), 'fde', split_axis=0, concat_ax...  7.67 us
    all_to_all x1, starting transfers between devices, body(): lax.all_to_all(shaped(send_query), 'fde', split_axis=0, concat_axis=0, ti...  7.25 us
  transfers between devices with their start and end apart: 8, of which 5 were waited for; matrix products, arithmetic and copies ran while one was open for 75% of the time, Pallas kernels for 0%

commit v1 on v0

v1 whole, which is shorter than its diff:
```python
import functools

import jax
import jax.numpy as jnp
from jax import lax
from jax.experimental import pallas as pl
from jax.experimental.pallas import tpu as pltpu
from jax.sharding import PartitionSpec as P

group = 8
chunk = 64
tile = 256


def maxsim_kernel(
    perm_ref, len_ref, level_ref, q_ref, seg_ref, p_ref, out_ref, packed, best
):
    pass_local, passage_slots, width = p_ref.shape
    levels_max = passage_slots // chunk
    rows = lax.broadcasted_iota(jnp.int32, (chunk, width), 0)

    def pack(i, carry):
        source = perm_ref[i]
        length = len_ref[i]
        head = p_ref[source, 0:1, :].astype(jnp.float32)
        for level in range(levels_max):
            block = p_ref[source, level * chunk : (level + 1) * chunk, :].astype(jnp.float32)
            block = jnp.where(rows + level * chunk < length, block, head)
            packed[i // group, level, i % group] = block.astype(jnp.bfloat16)
        return carry

    lax.fori_loop(0, pass_local, pack, 0)

    tiles = q_ref.shape[0] // tile
    out_ref[...] = jnp.zeros_like(out_ref)

    def one_tile(t, carry):
        vectors = q_ref[pl.ds(pl.multiple_of(t * tile, tile), tile), :]
        for g in range(pass_local // group):

            def step(level, acc):
                block = packed[g, level].reshape(group * chunk, width)
                similarity = lax.dot_general(
                    block, vectors, (((1,), (1,)), ((), ())), preferred_element_type=jnp.float32
                )
                similarity = similarity.reshape(group, chunk // 8, 8, tile)
                return jnp.maximum(acc, jnp.max(similarity, axis=1))

            acc = lax.fori_loop(
                0, level_ref[g], step, jnp.full((group, 8, tile), -3.0e38, jnp.float32)
            )
            found = jnp.max(acc, axis=1)
            for i in range(group):
                best[pl.ds(perm_ref[g * group + i], 1), :] = found[i : i + 1, :]
        queries = lax.broadcasted_iota(jnp.int32, (out_ref.shape[0], tile), 0)
        segment = seg_ref[pl.ds(t, 1), :]
        chosen = (queries == segment).astype(jnp.float32)
        out_ref[...] += lax.dot_general(
            chosen,
            best[...],
            (((1,), (1,)), ((), ())),
            preferred_element_type=jnp.float32,
            precision=lax.Precision.HIGHEST,
        )
        return carry

    lax.fori_loop(0, tiles, one_tile, 0)


def maxsim(tokens, segments, queries, passage_tokens, perm, lengths, levels):
    pass_local, passage_slots, width = passage_tokens.shape
    smem = pl.BlockSpec(memory_space=pltpu.SMEM)
    vmem = pl.BlockSpec(memory_space=pltpu.VMEM)
    return pl.pallas_call(
        maxsim_kernel,
        out_shape=jax.ShapeDtypeStruct((queries, pass_local), jnp.float32),
        in_specs=[smem, smem, smem, vmem, vmem, vmem],
        out_specs=vmem,
        scratch_shapes=[
            pltpu.VMEM((pass_local // group, passage_slots // chunk, group, chunk, width), jnp.bfloat16),
            pltpu.VMEM((pass_local, tile), jnp.float32),
        ],
        compiler_params=pltpu.CompilerParams(vmem_limit_bytes=40 * 1024 * 1024),
    )(perm, lengths, levels, tokens, segments, passage_tokens)


def body(
    query_fixed_encoding,
    passage_fde,
    query_tokens,
    query_token_totals,
    passage_tokens,
    passage_lengths,
    candidates,
):
    groups = lax.axis_size("fde")
    shards = lax.axis_size("pas")
    query_local, slots, width = query_tokens.shape
    pass_local = passage_tokens.shape[0]
    queries = groups * query_local

    live = lax.broadcasted_iota(jnp.int32, (query_local, slots, 1), 1) < query_token_totals[:, None, None]
    masked = jnp.where(live, query_tokens, jnp.bfloat16(0)).reshape(query_local * slots, width)
    tokens = lax.all_gather(masked, "fde", axis=0, tiled=True)

    incomplete = jnp.einsum(
        "qf,pf->qp", query_fixed_encoding, passage_fde, preferred_element_type=jnp.float32
    )
    fde_scores = lax.psum_scatter(incomplete, "fde", scatter_dimension=0, tiled=True)

    ids = jnp.arange(pass_local, dtype=jnp.int32)
    longer = (passage_lengths[None, :] > passage_lengths[:, None]) | (
        (passage_lengths[None, :] == passage_lengths[:, None]) & (ids[None, :] < ids[:, None])
    )
    rank = jnp.sum(longer.astype(jnp.int32), axis=1)
    placed = rank[None, :] == ids[:, None]
    perm = jnp.sum(jnp.where(placed, ids[None, :], 0), axis=1)
    lengths = jnp.sum(jnp.where(placed, passage_lengths[None, :], 0), axis=1)
    levels = (lengths[::group] + (chunk - 1)) // chunk
    segments = (jnp.arange(queries * slots, dtype=jnp.int32) // slots).reshape(-1, tile)

    table = maxsim(tokens, segments, queries, passage_tokens, perm, lengths, levels)
    back = lax.all_to_all(
        table.reshape(groups, query_local, pass_local), "fde", split_axis=0, concat_axis=0, tiled=True
    )
    back = lax.all_gather(back, "pas", axis=1)
    whole = jnp.transpose(back, (2, 0, 1, 3)).reshape(query_local, groups * shards * pass_local)
    every = jnp.arange(whole.shape[1], dtype=jnp.int32)
    rerank = jnp.sum(
        jnp.where(candidates[:, :, None] == every[None, None, :], whole[:, None, :], jnp.float32(0)), axis=2
    )
    rerank = rerank / query_token_totals.astype(jnp.float32)[:, None]
    return fde_scores, rerank


def solution(mesh):
    return jax.shard_map(
        body,
        mesh=mesh,
        in_specs=(
            P(None, "fde"),
            P("pas", "fde"),
            P("fde", None, None),
            P("fde"),
            P(("fde", "pas"), None, None),
            P(("fde", "pas")),
            P("fde", "pas"),
        ),
        out_specs=(P("fde", "pas"), P("fde", "pas")),
        check_vma=False,
    )
```

time: 313 us -> 188 us (0.60)
  local copies, waits for them, and re-layouts: 160 us -> 4.53 us
  waiting for transfers between devices: 19.6 us -> 99.4 us
  matrix products: 71.4 us -> 1 us
  Pallas kernels: 0 us -> 44.4 us
  starting transfers between devices: 28.1 us -> 12.5 us
  other arithmetic: 9.27 us -> 5.98 us
    gather x50 -> x0, local copies, waits for them, and re-layouts: 142 us -> none  [the longest x12 95.8 us: maxsim_block(): corpus_texts = jnp.take(passage_tokens, local_ids, axis=0)]
    dot_general x12 -> x0, matrix products: 69.4 us -> none  [maxsim_block(): jnp.einsum('zxg,zwg->zxw', token_vectors, corpus_texts, preferred_element...]
    reduce_scatter x0 -> x1, waiting for transfers between devices: none -> 52.4 us  [body(): lax.psum_scatter(incomplete, 'fde', scatter_dimension=0, tiled=True)]
    pallas_call x0 -> x1, Pallas kernels: none -> 44.4 us  [maxsim(): pl.pallas_call(maxsim_kernel, out_shape=jax.ShapeDtypeStruct((queries, pa...]
    all_gather x1, waiting for transfers between devices: 0.01 us -> 41.5 us  [body(): tokens = lax.all_gather(masked, 'fde', axis=0, tiled=True)]
    all_to_all x6 -> x1, starting transfers between devices: 28 us -> 12.5 us  [body(): lax.all_to_all(table.reshape(groups, query_local, pass_local), 'fde', spl...]
    all_to_all x6 -> x1, waiting for transfers between devices: 18.8 us -> 5.46 us  [body(): lax.all_to_all(table.reshape(groups, query_local, pass_local), 'fde', spl...]
    unnamed x1 -> x0, blocking collectives: 8.54 us -> none
  transfers between devices with their start and end apart: 8 -> 3, of which waited for: 5 -> 3; matrix products, arithmetic and copies ran while one was open for 75% -> 3% of each run, Pallas kernels for 0% -> 0%
where the time goes in v1:
time: 188 us
  waiting for transfers between devices  99.4 us (53%)
  Pallas kernels  44.4 us (24%)
  between operations  14.1 us (8%)
  starting transfers between devices  12.5 us (7%)
  blocking collectives  6.08 us (3%)
  other arithmetic  5.98 us (3%)
  local copies, waits for them, and re-layouts  4.53 us (2%)
    reduce_scatter x1, waiting for transfers between devices, body(): lax.psum_scatter(incomplete, 'fde', scatter_dimension=0, tiled=True)  52.4 us
    pallas_call x1, Pallas kernels, maxsim(): pl.pallas_call(maxsim_kernel, out_shape=jax.ShapeDtypeStruct((queries, pa...  44.4 us
    all_gather x1, waiting for transfers between devices, body(): tokens = lax.all_gather(masked, 'fde', axis=0, tiled=True)  41.5 us
    all_to_all x1, starting transfers between devices, body(): lax.all_to_all(table.reshape(groups, query_local, pass_local), 'fde', spl...  12.5 us
    all_gather x1, blocking collectives, body(): back = lax.all_gather(back, 'pas', axis=1)  6.08 us
    all_to_all x1, waiting for transfers between devices, body(): lax.all_to_all(table.reshape(groups, query_local, pass_local), 'fde', spl...  5.46 us
  transfers between devices with their start and end apart: 3, of which 3 were waited for; matrix products, arithmetic and copies ran while one was open for 3% of the time, Pallas kernels for 0%

profile of v1, /device:TPU:0, one launch (start us, length us, event | category | flops | bytes accessed | tf_op | source)
XLA Modules:
  0.0 188.0 jit_solution(205899170498506421)
XLA Ops:
  7.2 0.0 copy-start
  7.2 0.0 copy-start.3
  7.2 0.0 all-gather.3.cloned.1.call-start
  7.2 0.8 iota_compare_fusion.3
  8.0 1.7 broadcast_select_fusion
  9.7 0.0 all-gather.3.cloned.1.call-update
  9.7 0.9 convert_reduce_fusion
  10.7 0.8 select_reduce_fusion.1
  11.4 0.1 slice.3
  11.6 41.5 %all-gather.3.cloned.1.call-done.q_ref = bf16[4096,128]{1,0:T(8,128)(2,1)} async-done(((bf16[512,128]{1,0:T(8,128)(2,1)}), bf16[4096,128]{1,0:T(8,128)(2,1)}) %all-gather.3.cloned.1.call-update) | async-done | bytes 1048592 | tf_op jit(solution)/shard_map/all_gather | solution.py:104
  53.0 1.6 copy-done.1
  54.6 1.2 copy-done.2
  55.9 44.4 %shard_map.86 = f32[128,32]{1,0:T(8,128)S(1)} custom-call(s32[32]{0:T(128)S(1)} %get-tuple-element.3.perm_ref, s32[32]{0:T(128)S(1)} %get-tuple-element.2.len_ref, s32[4]{0:T(128)S(1)} %and_select_fusion.level_ref, bf16[4096,128]{1,0:T(8,128)(2,1)S(1)} %copy-done.2, s32[16,256]{1,0:T(8,128)S(1)} %add_select_fusion.seg_ref, bf16[32,256,128]{2,1,0:T(8,128)(2,1)S(1)} %copy-done.1), custom_call_target="tpu_custom_call" | custom-call | tf_op jit(solution)/shard_map/pallas_call | solution.py:74
  100.2 0.0 copy-start.4
  100.2 0.7 reshape.49
  100.9 12.5 %all-to-all-start = ((f32[8,1,512]{2,1,0:T(1,128)}), f32[8,1,512]{2,1,0:T(1,128)S(1)}, u32[]{:S(2)}, u32[]{:S(2)}) async-start(f32[8,1,512]{2,1,0:T(1,128)} %reshape.49), calls=%async_computation.1 | async-start | bytes 32768 | tf_op jit(solution)/shard_map/all_to_all | solution.py:123
  113.4 0.0 reduce-scatter.2.cloned.1.call-start
  113.4 0.0 copy-done
  113.5 1.0 fusion.5
  114.5 0.0 reduce-scatter.2.cloned.1.call-update
  114.5 0.0 copy-done.5
  114.5 5.5 %all-to-all-done = f32[8,1,512]{2,1,0:T(1,128)S(1)} async-done(((f32[8,1,512]{2,1,0:T(1,128)}), f32[8,1,512]{2,1,0:T(1,128)S(1)}, u32[]{:S(2)}, u32[]{:S(2)}) %all-to-all-start) | async-done | bytes 16416 | tf_op jit(solution)/shard_map/all_to_all | solution.py:123
  120.0 0.5 broadcast.67
  120.5 0.7 reduce
  121.2 0.1 reshape.50
  121.3 6.1 %all-gather = f32[8,64,32]{2,1,0:T(8,128)S(1)} all-gather(f32[8,16,32]{2,1,0:T(8,128)S(1)} %reshape.50), channel_id=2, replica_groups=mesh['fde'=8,'pas'=4] {'pas'}, dimensions={1}, use_global_device_ids=true | all-gather | bytes 81920 | tf_op jit(solution)/shard_map/all_gather | solution.py:126
  127.3 0.1 copy.10
  127.4 0.2 broadcast_in_dim.57
  127.7 0.0 copy-done.4
  127.7 0.4 select_reduce_fusion
  128.1 0.7 broadcast_divide_fusion
  128.8 52.4 %reduce-scatter.2.cloned.1.call-done = f32[16,256]{1,0:T(8,128)} async-done(((f32[128,256]{1,0:T(8,128)}), f32[16,256]{1,0:T(8,128)}) %reduce-scatter.2.cloned.1.call-update) | async-done | bytes 16400 | tf_op jit(solution)/shard_map/reduce_scatter | solution.py:109
  (7 shorter events, 0.0 us)
Async XLA Ops:
  7.2 106.3 %copy-start = (bf16[256,1280]{1,0:T(8,128)(2,1)S(1)}, bf16[256,1280]{1,0:T(8,128)(2,1)}, u32[]{:S(2)}) copy-start(bf16[256,1280]{1,0:T(8,128)(2,1)} %param.8) | copy-start | bytes 1966084
  7.2 106.3 %copy-start.3 = (bf16[128,1280]{1,0:T(8,128)(2,1)S(1)}, bf16[128,1280]{1,0:T(8,128)(2,1)}, u32[]{:S(2)}) copy-start(bf16[128,1280]{1,0:T(8,128)(2,1)} %param.7) | copy-start | bytes 983044
  7.2 45.9 %all-gather.3.cloned.1.call-start = ((), (), s32[]{:S(2)}) async-start(), calls=%async_computation.3 | async-start | bytes 1179648 | tf_op jit(solution)/shard_map/all_gather | solution.py:104
  53.0 1.6 copy-start.1
  54.6 1.2 copy-start.2
  55.9 58.6 %copy-start.5 = (s32[16]{0:T(128)S(1)}, s32[16]{0:T(128)}, u32[]{:S(2)}) copy-start(s32[16]{0:T(128)} %param.10) | copy-start | bytes 196
  100.2 27.4 %copy-start.4 = (s32[16,32]{1,0:T(8,128)S(1)}, s32[16,32]{1,0:T(8,128)}, u32[]{:S(2)}) copy-start(s32[16,32]{1,0:T(8,128)} %param.13) | copy-start | bytes 6148
  100.9 19.0 %all-to-all-start = ((f32[8,1,512]{2,1,0:T(1,128)}), f32[8,1,512]{2,1,0:T(1,128)S(1)}, u32[]{:S(2)}, u32[]{:S(2)}) async-start(f32[8,1,512]{2,1,0:T(1,128)} %reshape.49), calls=%async_computation.1 | async-start | bytes 32768 | tf_op jit(solution)/shard_map/all_to_all | solution.py:123
  113.4 67.8 %reduce-scatter.2.cloned.1.call-start = ((), (), s32[]{:S(2)}) async-start(), calls=%async_computation.2 | async-start | bytes 147456 | tf_op jit(solution)/shard_map/reduce_scatter | solution.py:109
Sparse Core Ops, SparseCore 0:
  10.1 42.8 all-gather.2
  118.1 62.9 reduce-scatter.1

commit v2 on v1

v2 whole, which is shorter than its diff:
```python
import functools

import jax
import jax.numpy as jnp
from jax import lax
from jax.experimental import pallas as pl
from jax.experimental.pallas import tpu as pltpu
from jax.sharding import PartitionSpec as P

MESH = pl.DeviceIdType.MESH
group = 8
chunk = 64
tile = 2048
part_tile = 256
lanes = 128


def maxsim_kernel(perm_ref, len_ref, level_ref, q_ref, p_ref, out_ref, packed, acc_ref, best, table):
    pass_local, passage_slots, width = p_ref.shape
    slots = q_ref.shape[0] // table.shape[0]
    levels_max = passage_slots // chunk
    rows = lax.broadcasted_iota(jnp.int32, (chunk, width), 0)

    def pack(i, carry):
        source = perm_ref[i]
        length = len_ref[i]
        head = p_ref[source, 0:1, :].astype(jnp.float32)
        for level in range(levels_max):
            block = p_ref[source, level * chunk : (level + 1) * chunk, :].astype(jnp.float32)
            block = jnp.where(rows + level * chunk < length, block, head)
            packed[i // group, level, i % group] = block.astype(jnp.bfloat16)
        return carry

    lax.fori_loop(0, pass_local, pack, 0)
    per_tile = tile // slots
    chosen = (
        lax.broadcasted_iota(jnp.int32, (per_tile, tile), 0)
        == lax.broadcasted_iota(jnp.int32, (per_tile, tile), 1) // slots
    ).astype(jnp.float32)

    def one_tile(t, carry):
        start = pl.multiple_of(t * tile, tile)
        for g in range(pass_local // group):
            acc_ref[...] = jnp.full(acc_ref.shape, -3.0e38, jnp.float32)

            def step(level, carry):
                block = packed[g, level].reshape(group * chunk, width)
                for s in range(0, tile, part_tile):
                    vectors = q_ref[pl.ds(pl.multiple_of(start + s, part_tile), part_tile), :]
                    similarity = lax.dot_general(
                        block, vectors, (((1,), (1,)), ((), ())), preferred_element_type=jnp.float32
                    )
                    found = jnp.max(similarity.reshape(group, chunk // 8, 8, part_tile), axis=1)
                    acc_ref[:, :, s : s + part_tile] = jnp.maximum(
                        acc_ref[:, :, s : s + part_tile], found
                    )
                return carry

            lax.fori_loop(0, level_ref[g], step, 0)
            found = jnp.max(acc_ref[...], axis=1)
            for i in range(group):
                best[pl.ds(perm_ref[g * group + i], 1), :] = found[i : i + 1, :]
        table[pl.ds(pl.multiple_of(t * per_tile, per_tile), per_tile), :] = lax.dot_general(
            chosen,
            best[...],
            (((1,), (1,)), ((), ())),
            preferred_element_type=jnp.float32,
            precision=lax.Precision.HIGHEST,
        )
        return carry

    lax.fori_loop(0, q_ref.shape[0] // tile, one_tile, 0)
    groups = out_ref.shape[0]
    query_local = table.shape[0] // groups
    for g in range(groups):
        for c in range(query_local // 8):
            first = g * query_local + c * 8
            out_ref[g, :, c * pass_local : (c + 1) * pass_local] = table[first : first + 8, :]


def maxsim(tokens, groups, slots, passage_tokens, perm, lengths, levels):
    pass_local, passage_slots, width = passage_tokens.shape
    smem = pl.BlockSpec(memory_space=pltpu.SMEM)
    vmem = pl.BlockSpec(memory_space=pltpu.VMEM)
    return pl.pallas_call(
        maxsim_kernel,
        out_shape=jax.ShapeDtypeStruct((groups, 8, lanes), jnp.float32),
        in_specs=[smem, smem, smem, vmem, vmem],
        out_specs=vmem,
        scratch_shapes=[
            pltpu.VMEM((pass_local // group, passage_slots // chunk, group, chunk, width), jnp.bfloat16),
            pltpu.VMEM((group, 8, tile), jnp.float32),
            pltpu.VMEM((pass_local, tile), jnp.float32),
            pltpu.VMEM((tokens.shape[0] // slots, pass_local), jnp.float32),
        ],
        compiler_params=pltpu.CompilerParams(vmem_limit_bytes=40 * 1024 * 1024),
        name="maxsim",
    )(perm, lengths, levels, tokens, passage_tokens)


def axis_pair(here, there):
    return {"fde": here, "pas": there}


def gather_kernel(
    groups, shards, totals_ref, qfe_ref, pfde_ref, tok_ref, out_ref, fde_ref,
    part, landed, send_a, recv_a, send_b, recv_b, send_c, recv_c, send_s, recv_s,
):
    f = lax.axis_index("fde")
    p = lax.axis_index("pas")
    query_local, slots, width = tok_ref.shape
    half = shards // 2
    core = lax.rem(p, 2)
    other = p + 1 - 2 * core
    rows = query_local * slots // shards

    barrier = pltpu.get_barrier_semaphore()
    for d in range(1, groups):
        pl.semaphore_signal(barrier, inc=1, device_id=axis_pair(lax.rem(f + d, groups), p), device_id_type=MESH)
    for e in range(1, half):
        pl.semaphore_signal(barrier, inc=1, device_id=axis_pair(f, lax.rem(p + 2 * e, shards)), device_id_type=MESH)
    pl.semaphore_signal(barrier, inc=1, device_id=axis_pair(f, other), device_id_type=MESH)

    slot = lax.broadcasted_iota(jnp.int32, (slots, width), 0)
    for q in range(query_local):
        block = tok_ref[q].astype(jnp.float32)
        block = jnp.where(slot < totals_ref[q], block, jnp.float32(0))
        out_ref[f, q * slots : (q + 1) * slots, :] = block.astype(jnp.bfloat16)
    pl.semaphore_wait(barrier, groups - 1 + half)

    def piece(group, owner):
        place = lax.rem(owner, 2) * half + owner // 2
        return out_ref.at[group, pl.ds(pl.multiple_of(place * rows, rows), rows), :]

    first = []
    for d in range(1, groups):
        copy = pltpu.make_async_remote_copy(
            src_ref=piece(f, p), dst_ref=piece(f, p), send_sem=send_a.at[d], recv_sem=recv_a.at[d],
            device_id=axis_pair(lax.rem(f + d, groups), p), device_id_type=MESH,
        )
        copy.start()
        first.append(copy)

    for g in range(groups):
        q = qfe_ref[g * query_local : (g + 1) * query_local, :]
        part[g] = lax.dot_general(
            q, pfde_ref[...], (((1,), (1,)), ((), ())), preferred_element_type=jnp.float32
        )
    sums = []
    for d in range(1, groups):
        g = lax.rem(f + d, groups)
        copy = pltpu.make_async_remote_copy(
            src_ref=part.at[g], dst_ref=landed.at[d], send_sem=send_s.at[d], recv_sem=recv_s.at[d],
            device_id=axis_pair(g, p), device_id_type=MESH,
        )
        copy.start()
        sums.append(copy)

    second = []
    for d in range(1, groups):
        first[d - 1].wait_recv()
        g = lax.rem(f - d + groups, groups)
        for e in range(1, half):
            copy = pltpu.make_async_remote_copy(
                src_ref=piece(g, p), dst_ref=piece(g, p), send_sem=send_b.at[d, e], recv_sem=recv_b.at[d, e],
                device_id=axis_pair(f, lax.rem(p + 2 * e, shards)), device_id_type=MESH,
            )
            copy.start()
            second.append(copy)
    third = []
    for d in range(1, groups):
        g = lax.rem(f - d + groups, groups)
        for e in range(1, half):
            second[(d - 1) * (half - 1) + e - 1].wait_recv()
        mine = out_ref.at[g, pl.ds(pl.multiple_of(core * (half * rows), half * rows), half * rows), :]
        copy = pltpu.make_async_remote_copy(
            src_ref=mine, dst_ref=mine, send_sem=send_c.at[d], recv_sem=recv_c.at[d],
            device_id=axis_pair(f, other), device_id_type=MESH,
        )
        copy.start()
        third.append(copy)

    total = part[f]
    for d in range(1, groups):
        sums[d - 1].wait_recv()
        total = total + landed[d]
    fde_ref[...] = total
    for copy in third:
        copy.wait_recv()
    for copy in first + second + third + sums:
        copy.wait_send()


def gather(groups, shards, totals, query_fixed_encoding, passage_fde, query_tokens):
    query_local, slots, width = query_tokens.shape
    passages = passage_fde.shape[0]
    smem = pl.BlockSpec(memory_space=pltpu.SMEM)
    vmem = pl.BlockSpec(memory_space=pltpu.VMEM)
    half = shards // 2
    dma = pltpu.SemaphoreType.DMA
    return pl.pallas_call(
        functools.partial(gather_kernel, groups, shards),
        out_shape=(
            jax.ShapeDtypeStruct((groups, query_local * slots, width), jnp.bfloat16),
            jax.ShapeDtypeStruct((query_local, passages), jnp.float32),
        ),
        in_specs=[smem, vmem, vmem, vmem],
        out_specs=(vmem, vmem),
        scratch_shapes=[
            pltpu.VMEM((groups, query_local, passages), jnp.float32),
            pltpu.VMEM((groups, query_local, passages), jnp.float32),
            dma((groups,)), dma((groups,)),
            dma((groups, half)), dma((groups, half)),
            dma((groups,)), dma((groups,)),
            dma((groups,)), dma((groups,)),
        ],
        compiler_params=pltpu.CompilerParams(
            collective_id=0, has_side_effects=True, vmem_limit_bytes=40 * 1024 * 1024
        ),
        name="gather_tokens",
    )(totals, query_fixed_encoding, passage_fde, query_tokens)


def return_kernel(groups, shards, table_ref, out_ref, send_sem, recv_sem):
    f = lax.axis_index("fde")
    p = lax.axis_index("pas")
    me = f * shards + p
    owners = groups * shards
    barrier = pltpu.get_barrier_semaphore()

    def signal(d, carry):
        o = lax.rem(me + d, owners)
        pl.semaphore_signal(
            barrier, inc=1, device_id=axis_pair(o // shards, lax.rem(o, shards)), device_id_type=MESH
        )
        return carry

    lax.fori_loop(1, owners, signal, 0)
    out_ref[me] = table_ref[f]
    pl.semaphore_wait(barrier, owners - 1)

    def copy_to(d):
        o = lax.rem(me + d, owners)
        return pltpu.make_async_remote_copy(
            src_ref=table_ref.at[o // shards], dst_ref=out_ref.at[me],
            send_sem=send_sem.at[d], recv_sem=recv_sem.at[d],
            device_id=axis_pair(o // shards, lax.rem(o, shards)), device_id_type=MESH,
        )

    def start(d, carry):
        copy_to(d).start()
        return carry

    def finish(d, carry):
        copy_to(d).wait()
        return carry

    lax.fori_loop(1, owners, start, 0)
    lax.fori_loop(1, owners, finish, 0)


def send_back(groups, shards, table):
    owners = groups * shards
    vmem = pl.BlockSpec(memory_space=pltpu.VMEM)
    return pl.pallas_call(
        functools.partial(return_kernel, groups, shards),
        out_shape=jax.ShapeDtypeStruct((owners,) + table.shape[1:], table.dtype),
        in_specs=[vmem],
        out_specs=vmem,
        scratch_shapes=[pltpu.SemaphoreType.DMA((owners,)), pltpu.SemaphoreType.DMA((owners,))],
        compiler_params=pltpu.CompilerParams(collective_id=1, has_side_effects=True),
        name="send_back",
    )(table)


def body(
    query_fixed_encoding,
    passage_fde,
    query_tokens,
    query_token_totals,
    passage_tokens,
    passage_lengths,
    candidates,
):
    groups = lax.axis_size("fde")
    shards = lax.axis_size("pas")
    query_local, slots, width = query_tokens.shape
    pass_local = passage_tokens.shape[0]

    tokens, fde_scores = gather(
        groups, shards, query_token_totals, query_fixed_encoding, passage_fde, query_tokens
    )

    ids = jnp.arange(pass_local, dtype=jnp.int32)
    longer = (passage_lengths[None, :] > passage_lengths[:, None]) | (
        (passage_lengths[None, :] == passage_lengths[:, None]) & (ids[None, :] < ids[:, None])
    )
    rank = jnp.sum(longer.astype(jnp.int32), axis=1)
    placed = rank[None, :] == ids[:, None]
    perm = jnp.sum(jnp.where(placed, ids[None, :], 0), axis=1)
    lengths = jnp.sum(jnp.where(placed, passage_lengths[None, :], 0), axis=1)
    levels = (lengths[::group] + (chunk - 1)) // chunk

    table = maxsim(tokens.reshape(-1, width), groups, slots, passage_tokens, perm, lengths, levels)
    back = send_back(groups, shards, table)
    packs = query_local // 8
    whole = back[:, :, : packs * pass_local].reshape(groups * shards, 8, packs, pass_local)
    whole = jnp.transpose(whole, (2, 1, 0, 3)).reshape(query_local, groups * shards * pass_local)
    every = jnp.arange(whole.shape[1], dtype=jnp.int32)
    rerank = jnp.sum(
        jnp.where(candidates[:, :, None] == every[None, None, :], whole[:, None, :], jnp.float32(0)), axis=2
    )
    rerank = rerank / query_token_totals.astype(jnp.float32)[:, None]
    return fde_scores, rerank


def solution(mesh):
    return jax.shard_map(
        body,
        mesh=mesh,
        in_specs=(
            P(None, "fde"),
            P("pas", "fde"),
            P("fde", None, None),
            P("fde"),
            P(("fde", "pas"), None, None),
            P(("fde", "pas")),
            P("fde", "pas"),
        ),
        out_specs=(P("fde", "pas"), P("fde", "pas")),
        check_vma=False,
    )
```

time: 188 us -> 63.8 us (0.34)
  waiting for transfers between devices: 99.4 us -> 0 us
  between operations: 14.1 us -> 0.71 us
  starting transfers between devices: 12.5 us -> 0 us
  Pallas kernels: 44.4 us -> 52.6 us
  blocking collectives: 6.08 us -> 0 us
  local copies, waits for them, and re-layouts: 4.53 us -> 7.83 us
  other arithmetic: 5.98 us -> 2.78 us
    reduce_scatter x1 -> x0, waiting for transfers between devices: 52.4 us -> none  [body(): lax.psum_scatter(incomplete, 'fde', scatter_dimension=0, tiled=True)]
    all_gather x1 -> x0, waiting for transfers between devices: 41.5 us -> none  [body(): tokens = lax.all_gather(masked, 'fde', axis=0, tiled=True)]
    all_to_all x1 -> x0, starting transfers between devices: 12.5 us -> none  [body(): lax.all_to_all(table.reshape(groups, query_local, pass_local), 'fde', spl...]
    pallas_call x1 -> x3, Pallas kernels: 44.4 us -> 52.6 us  [the longest x1 22.2 us: maxsim(): pl.pallas_call(maxsim_kernel, out_shape=jax.ShapeDtypeStruct((groups, 8,...]
    all_gather x1 -> x0, blocking collectives: 6.08 us -> none  [body(): back = lax.all_gather(back, 'pas', axis=1)]
    all_to_all x1 -> x0, waiting for transfers between devices: 5.46 us -> none  [body(): lax.all_to_all(table.reshape(groups, query_local, pass_local), 'fde', spl...]
    unnamed x14 -> x17, local copies, waits for them, and re-layouts: 3.61 us -> 6.42 us
  transfers between devices with their start and end apart: 3 -> 0, of which waited for: 3 -> 0; matrix products, arithmetic and copies ran while one was open for 3% -> 0% of each run, Pallas kernels for 0% -> 0%
where the time goes in v2:
time: 63.8 us; the launch traced here: 63.9 us
  Pallas kernels  52.6 us (82%)
  local copies, waits for them, and re-layouts  7.83 us (12%)
  other arithmetic  2.78 us (4%)
  between operations  0.71 us (1%)
    pallas_call x1, Pallas kernels, maxsim(): pl.pallas_call(maxsim_kernel, out_shape=jax.ShapeDtypeStruct((groups, 8,...  22.2 us
    pallas_call x1, Pallas kernels, gather(): pl.pallas_call(functools.partial(gather_kernel, groups, shards), out_shap...  18.1 us
    pallas_call x1, Pallas kernels, send_back(): pl.pallas_call(functools.partial(return_kernel, groups, shards), out_shap...  12.3 us
    unnamed x17, local copies, waits for them, and re-layouts  6.42 us

profile of v2, /device:TPU:0, one launch (start us, length us, event | category | flops | bytes accessed | tf_op | source)
XLA Modules:
  0.0 63.9 jit_solution(5964364121742379030)
XLA Ops:
  0.6 0.0 copy-start.1
  0.6 1.1 %copy-done.1 = bf16[256,1280]{1,0:T(8,128)(2,1)S(1)} copy-done((bf16[256,1280]{1,0:T(8,128)(2,1)S(1)}, bf16[256,1280]{1,0:T(8,128)(2,1)}, u32[]{:S(2)}) %copy-start.1) | copy-done | bytes 655384
  1.7 0.0 copy-start.2
  1.7 1.0 %copy-done.2 = bf16[128,1280]{1,0:T(8,128)(2,1)S(1)} copy-done((bf16[128,1280]{1,0:T(8,128)(2,1)S(1)}, bf16[128,1280]{1,0:T(8,128)(2,1)}, u32[]{:S(2)}) %copy-start.2) | copy-done | bytes 327704
  2.7 0.0 copy-start.4
  2.7 0.9 %copy-done.4 = bf16[16,32,128]{2,1,0:T(8,128)(2,1)S(1)} copy-done((bf16[16,32,128]{2,1,0:T(8,128)(2,1)S(1)}, bf16[16,32,128]{2,1,0:T(8,128)(2,1)}, u32[]{:S(2)}) %copy-start.4) | copy-done | bytes 131096
  3.6 0.0 copy-start.5
  3.6 0.7 %copy-done.5 = s32[16]{0:T(128)S(1)} copy-done((s32[16]{0:T(128)S(1)}, s32[16]{0:T(128)}, u32[]{:S(2)}) %copy-start.5) | copy-done | bytes 88
  4.3 18.1 %gather_tokens.1 = (bf16[8,512,128]{2,1,0:T(8,128)(2,1)S(1)}, f32[16,256]{1,0:T(8,128)S(1)}) custom-call(s32[16]{0:T(128)S(1)} %copy-done.5, bf16[128,1280]{1,0:T(8,128)(2,1)S(1)} %copy-done.2, bf16[256,1280]{1,0:T(8,128)(2,1)S(1)} %copy-done.1, bf16[16,32,128]{2,1,0:T(8,128)(2,1)S(1)} %copy-done.4), custom_call_target="tpu_custom_call" | custom-call | tf_op jit(solution)/shard_map/gather_tokens/pallas_call | solution.py:201
  22.3 0.9 %convert_reduce_fusion = s32[32]{0:T(128)S(1)} fusion(s32[32]{0:T(128)} %param.12), kind=kLoop, calls=%fused_computation.6 | loop fusion | flops 7136 | bytes 256 | tf_op jit(solution)/shard_map/reduce_sum | solution.py:298
  23.3 0.8 %select_reduce_fusion.1 = (s32[32]{0:T(128)S(1)}, s32[32]{0:T(128)S(1)}) fusion(s32[32]{0:T(128)S(1)} %convert_reduce_fusion, s32[32]{0:T(128)} %param.12), kind=kLoop, calls=%fused_computation.3 | loop fusion | flops 5056 | bytes 512 | tf_op jit(solution)/shard_map/reduce_sum | solution.py:301
  24.0 0.1 slice.6
  24.1 0.0 copy-start
  24.2 1.6 %copy-done = bf16[32,256,128]{2,1,0:T(8,128)(2,1)S(1)} copy-done((bf16[32,256,128]{2,1,0:T(8,128)(2,1)S(1)}, bf16[32,256,128]{2,1,0:T(8,128)(2,1)}, u32[]{:S(2)}) %copy-start) | copy-done | bytes 2097176
  25.7 0.0 copy-start.7
  25.7 0.0 copy-start.6
  25.7 22.2 %maxsim.1.table_ref = f32[8,8,128]{2,1,0:T(8,128)S(1)} custom-call(s32[32]{0:T(128)S(1)} %get-tuple-element.7.perm_ref, s32[32]{0:T(128)S(1)} %get-tuple-element.6.len_ref, s32[4]{0:T(128)S(1)} %and_select_fusion.level_ref, bf16[4096,128]{1,0:T(8,128)(2,1)S(1)} %bitcast.7, bf16[32,256,128]{2,1,0:T(8,128)(2,1)S(1)} %copy-done), custom_call_target="tpu_custom_call" | custom-call | tf_op jit(solution)/shard_map/maxsim/pallas_call | solution.py:85
  48.0 0.0 copy-start.3
  48.0 0.6 copy-done.3
  48.6 12.3 %send_back.1 = f32[32,8,128]{2,1,0:T(8,128)} custom-call(f32[8,8,128]{2,1,0:T(8,128)} %copy-done.3), custom_call_target="tpu_custom_call" | custom-call | tf_op jit(solution)/shard_map/send_back/pallas_call | solution.py:265
  60.9 1.1 %reshape.17 = f32[32,8,2,32]{3,2,1,0:T(2,128)S(1)} reshape(f32[32,8,64]{2,1,0:T(8,128)} %bitcast.9) | data formatting | bytes 131072 | tf_op jit(solution)/shard_map/reshape | solution.py:307
  62.0 0.1 copy.12
  62.1 0.1 broadcast_in_dim.42
  62.2 0.0 copy-done.7
  62.2 0.4 select_reduce_fusion
  62.6 0.0 copy-done.6
  62.6 0.7 %broadcast_divide_fusion = f32[16,32]{1,0:T(8,128)} fusion(f32[16,32]{1,0:T(8,128)S(1)} %select_reduce_fusion, f32[16]{0:T(128)S(1)} %convert_element_type.7), kind=kLoop, calls=%fused_computation.10 | loop fusion | flops 512 | bytes 4160 | tf_op jit(solution)/shard_map/div | solution.py:313
  63.3 0.6 copy.14
  (2 shorter events, 0.0 us)
Async XLA Ops:
  0.6 1.1 %copy-start.1 = (bf16[256,1280]{1,0:T(8,128)(2,1)S(1)}, bf16[256,1280]{1,0:T(8,128)(2,1)}, u32[]{:S(2)}) copy-start(bf16[256,1280]{1,0:T(8,128)(2,1)} %pfde_ref.1) | copy-start | bytes 1966084
  1.7 1.0 %copy-start.2 = (bf16[128,1280]{1,0:T(8,128)(2,1)S(1)}, bf16[128,1280]{1,0:T(8,128)(2,1)}, u32[]{:S(2)}) copy-start(bf16[128,1280]{1,0:T(8,128)(2,1)} %qfe_ref.1) | copy-start | bytes 983044
  2.7 0.9 %copy-start.4 = (bf16[16,32,128]{2,1,0:T(8,128)(2,1)S(1)}, bf16[16,32,128]{2,1,0:T(8,128)(2,1)}, u32[]{:S(2)}) copy-start(bf16[16,32,128]{2,1,0:T(8,128)(2,1)} %tok_ref.1) | copy-start | bytes 393220
  3.6 0.7 %copy-start.5 = (s32[16]{0:T(128)S(1)}, s32[16]{0:T(128)}, u32[]{:S(2)}) copy-start(s32[16]{0:T(128)} %totals_ref.1) | copy-start | bytes 196
  24.1 1.6 %copy-start = (bf16[32,256,128]{2,1,0:T(8,128)(2,1)S(1)}, bf16[32,256,128]{2,1,0:T(8,128)(2,1)}, u32[]{:S(2)}) copy-start(bf16[32,256,128]{2,1,0:T(8,128)(2,1)} %p_ref.1) | copy-start | bytes 6291460
  25.7 36.5 %copy-start.7 = (s32[16,32]{1,0:T(8,128)S(1)}, s32[16,32]{1,0:T(8,128)}, u32[]{:S(2)}) copy-start(s32[16,32]{1,0:T(8,128)} %param.13) | copy-start | bytes 6148
  25.7 36.9 %copy-start.6 = (s32[16]{0:T(128)S(1)}, s32[16]{0:T(128)}, u32[]{:S(2)}) copy-start(s32[16]{0:T(128)} %totals_ref.1) | copy-start | bytes 196
  48.0 0.6 copy-start.3

commit v3 on v1

v3 whole, which is shorter than its diff:
```python
import functools

import jax
import jax.numpy as jnp
from jax import lax
from jax.experimental import pallas as pl
from jax.experimental.pallas import tpu as pltpu
from jax.sharding import PartitionSpec as P

MESH = pl.DeviceIdType.MESH
block = 16
part_tile = 256
lanes = 128


def axis_pair(here, there):
    return {"fde": here, "pas": there}


def kernel(
    groups, shards, totals_ref, len_ref, qfe_hbm, pfde_hbm, tok_hbm, pass_hbm, out_ref, fde_ref,
    qfe, pfde, own, packed, tokens, best, table, part, landed,
    load, send_a, recv_a, send_b, recv_b, send_c, recv_c, send_s, recv_s, send_r, recv_r,
):
    f = lax.axis_index("fde")
    p = lax.axis_index("pas")
    me = f * shards + p
    owners = groups * shards
    query_local, slots, width = own.shape
    pass_local, passage_slots, _ = packed.shape
    half = shards // 2
    core = lax.rem(p, 2)
    other = p + 1 - 2 * core
    rows = query_local * slots // shards

    loads = [
        pltpu.make_async_copy(source, target, load.at[i])
        for i, (source, target) in enumerate(
            ((tok_hbm, own), (pass_hbm, packed), (pfde_hbm, pfde), (qfe_hbm, qfe))
        )
    ]
    for copy in loads:
        copy.start()

    barrier = pltpu.get_barrier_semaphore()

    def signal(d, carry):
        o = lax.rem(me + d, owners)
        pl.semaphore_signal(
            barrier, inc=1, device_id=axis_pair(o // shards, lax.rem(o, shards)), device_id_type=MESH
        )
        return carry

    lax.fori_loop(1, owners, signal, 0)

    loads[0].wait()
    slot = lax.broadcasted_iota(jnp.int32, (slots, width), 0)
    for q in range(query_local):
        vectors = own[q].astype(jnp.float32)
        vectors = jnp.where(slot < totals_ref[q], vectors, jnp.float32(0))
        tokens[f, q * slots : (q + 1) * slots, :] = vectors.astype(jnp.bfloat16)

    loads[1].wait()
    place = lax.broadcasted_iota(jnp.int32, (passage_slots, width), 0)

    def fill(i, carry):
        first = packed[i, 0:1, :].astype(jnp.float32)
        whole = jnp.where(place < len_ref[i], packed[i].astype(jnp.float32), first)
        packed[i] = whole.astype(jnp.bfloat16)
        return carry

    lax.fori_loop(0, pass_local, fill, 0)
    table[...] = jnp.zeros_like(table)
    pl.semaphore_wait(barrier, owners - 1)

    def piece(g, owner):
        at = lax.rem(owner, 2) * half + owner // 2
        return tokens.at[g, pl.ds(pl.multiple_of(at * rows, rows), rows), :]

    first = []
    for d in range(1, groups):
        copy = pltpu.make_async_remote_copy(
            src_ref=piece(f, p), dst_ref=piece(f, p), send_sem=send_a.at[d], recv_sem=recv_a.at[d],
            device_id=axis_pair(lax.rem(f + d, groups), p), device_id_type=MESH,
        )
        copy.start()
        first.append(copy)

    columns = query_local * slots
    chosen = (
        lax.broadcasted_iota(jnp.int32, (query_local, columns), 0)
        == lax.broadcasted_iota(jnp.int32, (query_local, columns), 1) // slots
    ).astype(jnp.float32)

    def score(g, d):
        def step(i, carry):
            passages = packed[pl.ds(i * block, block)].reshape(block * passage_slots, width)
            for s in range(0, columns, part_tile):
                similarity = lax.dot_general(
                    passages,
                    tokens[g, s : s + part_tile, :],
                    (((1,), (1,)), ((), ())),
                    preferred_element_type=jnp.float32,
                )
                found = jnp.max(similarity.reshape(block, passage_slots // 8, 8, part_tile), axis=1)
                best[i, :, s : s + part_tile] = jnp.max(found, axis=1)
            return carry

        lax.fori_loop(0, pass_local // block, step, 0)
        summed = lax.dot_general(
            chosen,
            best[...].reshape(pass_local, columns),
            (((1,), (1,)), ((), ())),
            preferred_element_type=jnp.float32,
            precision=lax.Precision.HIGHEST,
        )
        for c in range(query_local // 8):
            table[d, :, c * pass_local : (c + 1) * pass_local] = summed[c * 8 : (c + 1) * 8, :]

    def home(d, e):
        at = d * shards + e
        return pltpu.make_async_remote_copy(
            src_ref=table.at[d], dst_ref=out_ref.at[me],
            send_sem=send_r.at[at], recv_sem=recv_r.at[at],
            device_id=axis_pair(lax.rem(f - d + groups, groups), lax.rem(p + e, shards)),
            device_id_type=MESH,
        )

    def send_home(d, least):
        def go(e, carry):
            home(d, e).start()
            return carry

        lax.fori_loop(least, shards, go, 0)

    score(f, 0)
    out_ref[me] = table[0]
    send_home(0, 1)

    second = []
    for d in range(1, groups):
        first[d - 1].wait_recv()
        g = lax.rem(f - d + groups, groups)
        for e in range(1, half):
            copy = pltpu.make_async_remote_copy(
                src_ref=piece(g, p), dst_ref=piece(g, p), send_sem=send_b.at[d, e], recv_sem=recv_b.at[d, e],
                device_id=axis_pair(f, lax.rem(p + 2 * e, shards)), device_id_type=MESH,
            )
            copy.start()
            second.append(copy)

    loads[2].wait()
    loads[3].wait()
    for g in range(groups):
        part[g] = lax.dot_general(
            qfe[g * query_local : (g + 1) * query_local, :],
            pfde[...],
            (((1,), (1,)), ((), ())),
            preferred_element_type=jnp.float32,
        )

    third = []
    for d in range(1, groups):
        g = lax.rem(f - d + groups, groups)
        for e in range(1, half):
            second[(d - 1) * (half - 1) + e - 1].wait_recv()
        mine = tokens.at[g, pl.ds(pl.multiple_of(core * (half * rows), half * rows), half * rows), :]
        copy = pltpu.make_async_remote_copy(
            src_ref=mine, dst_ref=mine, send_sem=send_c.at[d], recv_sem=recv_c.at[d],
            device_id=axis_pair(f, other), device_id_type=MESH,
        )
        copy.start()
        third.append(copy)

    sums = []
    for d in range(1, groups):
        g = lax.rem(f + d, groups)
        copy = pltpu.make_async_remote_copy(
            src_ref=part.at[g], dst_ref=landed.at[d], send_sem=send_s.at[d], recv_sem=recv_s.at[d],
            device_id=axis_pair(g, p), device_id_type=MESH,
        )
        copy.start()
        sums.append(copy)

    def one_group(d, carry):
        g = lax.rem(f - d + groups, groups)
        mine = tokens.at[g, pl.ds(pl.multiple_of(core * (half * rows), half * rows), half * rows), :]
        pltpu.make_async_remote_copy(
            src_ref=mine, dst_ref=mine, send_sem=send_c.at[d], recv_sem=recv_c.at[d],
            device_id=axis_pair(f, other), device_id_type=MESH,
        ).wait_recv()
        score(g, d)
        send_home(d, 0)
        return carry

    lax.fori_loop(1, groups, one_group, 0)

    total = part[f]
    for d in range(1, groups):
        sums[d - 1].wait_recv()
        total = total + landed[d]
    fde_ref[...] = total
    for copy in first + second + third + sums:
        copy.wait_send()

    def finish(at, carry):
        home(at // shards, lax.rem(at, shards)).wait()
        return carry

    lax.fori_loop(1, owners, finish, 0)


def call(groups, shards, totals, lengths, qfe, pfde, query_tokens, passage_tokens):
    query_local, slots, width = query_tokens.shape
    pass_local, passage_slots, _ = passage_tokens.shape
    passages = pfde.shape[0]
    owners = groups * shards
    half = shards // 2
    smem = pl.BlockSpec(memory_space=pltpu.SMEM)
    vmem = pl.BlockSpec(memory_space=pltpu.VMEM)
    far = pl.BlockSpec(memory_space=pl.ANY)
    dma = pltpu.SemaphoreType.DMA
    bf16, f32 = jnp.bfloat16, jnp.float32
    columns = query_local * slots
    return pl.pallas_call(
        functools.partial(kernel, groups, shards),
        out_shape=(
            jax.ShapeDtypeStruct((owners, 8, lanes), f32),
            jax.ShapeDtypeStruct((query_local, passages), f32),
        ),
        in_specs=[smem, smem, far, far, far, far],
        out_specs=(vmem, vmem),
        scratch_shapes=[
            pltpu.VMEM(qfe.shape, bf16),
            pltpu.VMEM(pfde.shape, bf16),
            pltpu.VMEM(query_tokens.shape, bf16),
            pltpu.VMEM(passage_tokens.shape, bf16),
            pltpu.VMEM((groups, columns, width), bf16),
            pltpu.VMEM((pass_local // block, block, columns), f32),
            pltpu.VMEM((groups, 8, lanes), f32),
            pltpu.VMEM((groups, query_local, passages), f32),
            pltpu.VMEM((groups, query_local, passages), f32),
            dma((4,)),
            dma((groups,)), dma((groups,)),
            dma((groups, half)), dma((groups, half)),
            dma((groups,)), dma((groups,)),
            dma((groups,)), dma((groups,)),
            dma((owners,)), dma((owners,)),
        ],
        compiler_params=pltpu.CompilerParams(
            collective_id=0, has_side_effects=True, vmem_limit_bytes=40 * 1024 * 1024
        ),
        name="retrieve",
    )(totals, lengths, qfe, pfde, query_tokens, passage_tokens)


def body(
    query_fixed_encoding,
    passage_fde,
    query_tokens,
    query_token_totals,
    passage_tokens,
    passage_lengths,
    candidates,
):
    groups = lax.axis_size("fde")
    shards = lax.axis_size("pas")
    query_local, slots, width = query_tokens.shape
    pass_local = passage_tokens.shape[0]

    back, fde_scores = call(
        groups, shards, query_token_totals, passage_lengths,
        query_fixed_encoding, passage_fde, query_tokens, passage_tokens,
    )
    packs = query_local // 8
    whole = back[:, :, : packs * pass_local].reshape(groups * shards, 8, packs, pass_local)
    whole = jnp.transpose(whole, (2, 1, 0, 3)).reshape(query_local, groups * shards * pass_local)
    every = jnp.arange(whole.shape[1], dtype=jnp.int32)
    rerank = jnp.sum(
        jnp.where(candidates[:, :, None] == every[None, None, :], whole[:, None, :], jnp.float32(0)), axis=2
    )
    rerank = rerank / query_token_totals.astype(jnp.float32)[:, None]
    return fde_scores, rerank


def solution(mesh):
    return jax.shard_map(
        body,
        mesh=mesh,
        in_specs=(
            P(None, "fde"),
            P("pas", "fde"),
            P("fde", None, None),
            P("fde"),
            P(("fde", "pas"), None, None),
            P(("fde", "pas")),
            P("fde", "pas"),
        ),
        out_specs=(P("fde", "pas"), P("fde", "pas")),
        check_vma=False,
    )
```

time: 188 us -> 54.4 us (0.29)
  waiting for transfers between devices: 99.4 us -> 0 us
  between operations: 14.1 us -> 0.69 us
  starting transfers between devices: 12.5 us -> 0 us
  blocking collectives: 6.08 us -> 0 us
  other arithmetic: 5.98 us -> 1.09 us
  local copies, waits for them, and re-layouts: 4.53 us -> 6.89 us
    reduce_scatter x1 -> x0, waiting for transfers between devices: 52.4 us -> none  [body(): lax.psum_scatter(incomplete, 'fde', scatter_dimension=0, tiled=True)]
    all_gather x1 -> x0, waiting for transfers between devices: 41.5 us -> none  [body(): tokens = lax.all_gather(masked, 'fde', axis=0, tiled=True)]
    all_to_all x1 -> x0, starting transfers between devices: 12.5 us -> none  [body(): lax.all_to_all(table.reshape(groups, query_local, pass_local), 'fde', spl...]
    all_gather x1 -> x0, blocking collectives: 6.08 us -> none  [body(): back = lax.all_gather(back, 'pas', axis=1)]
    all_to_all x1 -> x0, waiting for transfers between devices: 5.46 us -> none  [body(): lax.all_to_all(table.reshape(groups, query_local, pass_local), 'fde', spl...]
    unnamed x14 -> x17, local copies, waits for them, and re-layouts: 3.61 us -> 6.47 us
  transfers between devices with their start and end apart: 3 -> 0, of which waited for: 3 -> 0; matrix products, arithmetic and copies ran while one was open for 3% -> 0% of each run, Pallas kernels for 0% -> 0%
where the time goes in v3:
time: 54.4 us; the launch traced here: 54.1 us
  Pallas kernels  45.4 us (83%)
  local copies, waits for them, and re-layouts  6.89 us (13%)
  other arithmetic  1.09 us (2%)
  between operations  0.69 us (1%)
    pallas_call x1, Pallas kernels, call(): pl.pallas_call(functools.partial(kernel, groups, shards), out_shape=(jax....  45.4 us
    unnamed x17, local copies, waits for them, and re-layouts  6.47 us

profile of v3, /device:TPU:0, one launch (start us, length us, event | category | flops | bytes accessed | tf_op | source)
XLA Modules:
  0.0 54.1 jit_solution(14293003452137376983)
XLA Ops:
  0.6 0.0 copy-start
  0.6 1.6 %copy-done = bf16[32,256,128]{2,1,0:T(8,128)(2,1)S(1)} copy-done((bf16[32,256,128]{2,1,0:T(8,128)(2,1)S(1)}, bf16[32,256,128]{2,1,0:T(8,128)(2,1)}, u32[]{:S(2)}) %copy-start) | copy-done | bytes 2097176
  2.2 0.0 copy-start.1
  2.2 1.1 %copy-done.1 = bf16[256,1280]{1,0:T(8,128)(2,1)S(1)} copy-done((bf16[256,1280]{1,0:T(8,128)(2,1)S(1)}, bf16[256,1280]{1,0:T(8,128)(2,1)}, u32[]{:S(2)}) %copy-start.1) | copy-done | bytes 655384
  3.3 0.0 copy-start.2
  3.3 1.0 %copy-done.2 = bf16[128,1280]{1,0:T(8,128)(2,1)S(1)} copy-done((bf16[128,1280]{1,0:T(8,128)(2,1)S(1)}, bf16[128,1280]{1,0:T(8,128)(2,1)}, u32[]{:S(2)}) %copy-start.2) | copy-done | bytes 327704
  4.3 0.0 copy-start.3
  4.3 0.9 %copy-done.3 = bf16[16,32,128]{2,1,0:T(8,128)(2,1)S(1)} copy-done((bf16[16,32,128]{2,1,0:T(8,128)(2,1)S(1)}, bf16[16,32,128]{2,1,0:T(8,128)(2,1)}, u32[]{:S(2)}) %copy-start.3) | copy-done | bytes 131096
  5.2 0.0 copy-start.4
  5.2 0.7 %copy-done.4 = s32[32]{0:T(128)S(1)} copy-done((s32[32]{0:T(128)S(1)}, s32[32]{0:T(128)}, u32[]{:S(2)}) %copy-start.4) | copy-done | bytes 152
  5.8 0.0 copy-start.5
  5.8 0.7 %copy-done.5 = s32[16]{0:T(128)S(1)} copy-done((s32[16]{0:T(128)S(1)}, s32[16]{0:T(128)}, u32[]{:S(2)}) %copy-start.5) | copy-done | bytes 88
  6.5 0.0 copy-start.7
  6.5 0.0 copy-start.6
  6.5 45.4 %retrieve.1 = (f32[32,8,128]{2,1,0:T(8,128)S(1)}, f32[16,256]{1,0:T(8,128)S(1)}) custom-call(s32[16]{0:T(128)S(1)} %copy-done.5, s32[32]{0:T(128)S(1)} %copy-done.4, bf16[128,1280]{1,0:T(8,128)(2,1)S(1)} %copy-done.2, bf16[256,1280]{1,0:T(8,128)(2,1)S(1)} %copy-done.1, bf16[16,32,128]{2,1,0:T(8,128)(2,1)S(1)} %copy-done.3, bf16[32,256,128]{2,1,0:T(8,128)(2,1)S(1)} %copy-done), custom_call_target="tpu_custom_call" | custom-call | tf_op jit(solution)/shard_map/retrieve/pallas_call | solution.py:225
  52.0 0.2 reshape.10
  52.2 0.1 copy.12
  52.3 0.1 broadcast_in_dim.17
  52.4 0.0 copy-done.7
  52.4 0.4 select_reduce_fusion
  52.8 0.0 copy-done.6
  52.8 0.7 %broadcast_divide_fusion = f32[16,32]{1,0:T(8,128)} fusion(f32[16,32]{1,0:T(8,128)S(1)} %select_reduce_fusion, f32[16]{0:T(128)S(1)} %convert_element_type.3), kind=kLoop, calls=%fused_computation.3 | loop fusion | flops 512 | bytes 4160 | tf_op jit(solution)/shard_map/div | solution.py:282
  53.5 0.6 %copy.14 = f32[16,256]{1,0:T(8,128)} copy(f32[16,256]{1,0:T(8,128)S(1)} %get-tuple-element.8) | data formatting | bytes 32768
  (1 shorter events, 0.0 us)
Async XLA Ops:
  0.6 1.6 %copy-start = (bf16[32,256,128]{2,1,0:T(8,128)(2,1)S(1)}, bf16[32,256,128]{2,1,0:T(8,128)(2,1)}, u32[]{:S(2)}) copy-start(bf16[32,256,128]{2,1,0:T(8,128)(2,1)} %pass_hbm.1) | copy-start | bytes 6291460
  2.2 1.1 %copy-start.1 = (bf16[256,1280]{1,0:T(8,128)(2,1)S(1)}, bf16[256,1280]{1,0:T(8,128)(2,1)}, u32[]{:S(2)}) copy-start(bf16[256,1280]{1,0:T(8,128)(2,1)} %pfde_hbm.1) | copy-start | bytes 1966084
  3.3 1.0 %copy-start.2 = (bf16[128,1280]{1,0:T(8,128)(2,1)S(1)}, bf16[128,1280]{1,0:T(8,128)(2,1)}, u32[]{:S(2)}) copy-start(bf16[128,1280]{1,0:T(8,128)(2,1)} %qfe_hbm.1) | copy-start | bytes 983044
  4.3 0.9 %copy-start.3 = (bf16[16,32,128]{2,1,0:T(8,128)(2,1)S(1)}, bf16[16,32,128]{2,1,0:T(8,128)(2,1)}, u32[]{:S(2)}) copy-start(bf16[16,32,128]{2,1,0:T(8,128)(2,1)} %tok_hbm.1) | copy-start | bytes 393220
  5.2 0.7 %copy-start.4 = (s32[32]{0:T(128)S(1)}, s32[32]{0:T(128)}, u32[]{:S(2)}) copy-start(s32[32]{0:T(128)} %len_ref.1) | copy-start | bytes 388
  5.8 0.7 %copy-start.5 = (s32[16]{0:T(128)S(1)}, s32[16]{0:T(128)}, u32[]{:S(2)}) copy-start(s32[16]{0:T(128)} %totals_ref.1) | copy-start | bytes 196
  6.5 45.9 %copy-start.7 = (s32[16,32]{1,0:T(8,128)S(1)}, s32[16,32]{1,0:T(8,128)}, u32[]{:S(2)}) copy-start(s32[16,32]{1,0:T(8,128)} %param.13) | copy-start | bytes 6148
  6.5 46.3 %copy-start.6 = (s32[16]{0:T(128)S(1)}, s32[16]{0:T(128)}, u32[]{:S(2)}) copy-start(s32[16]{0:T(128)} %totals_ref.1) | copy-start | bytes 196

commit v4 on v3

--- a/solution.py
+++ b/solution.py
@@ -60,6 +60,49 @@
         vectors = jnp.where(slot < totals_ref[q], vectors, jnp.float32(0))
         tokens[f, q * slots : (q + 1) * slots, :] = vectors.astype(jnp.bfloat16)
 
+    table[...] = jnp.zeros_like(table)
+    pl.semaphore_wait(barrier, owners - 1)
+
+    def piece(g, owner):
+        at = lax.rem(owner, 2) * half + owner // 2
+        return tokens.at[g, pl.ds(pl.multiple_of(at * rows, rows), rows), :]
+
+    def halves(g):
+        return tokens.at[g, pl.ds(pl.multiple_of(core * (half * rows), half * rows), half * rows), :]
+
+    def spread(d):
+        return pltpu.make_async_remote_copy(
+            src_ref=piece(f, p), dst_ref=piece(f, p), send_sem=send_a.at[d], recv_sem=recv_a.at[d],
+            device_id=axis_pair(lax.rem(f + d, groups), p), device_id_type=MESH,
+        )
+
+    def across(d, e):
+        g = lax.rem(f - d + groups, groups)
+        return pltpu.make_async_remote_copy(
+            src_ref=piece(g, p), dst_ref=piece(g, p), send_sem=send_b.at[d, e], recv_sem=recv_b.at[d, e],
+            device_id=axis_pair(f, lax.rem(p + 2 * e, shards)), device_id_type=MESH,
+        )
+
+    def to_core(d):
+        g = lax.rem(f - d + groups, groups)
+        return pltpu.make_async_remote_copy(
+            src_ref=halves(g), dst_ref=halves(g), send_sem=send_c.at[d], recv_sem=recv_c.at[d],
+            device_id=axis_pair(f, other), device_id_type=MESH,
+        )
+
+    def pass_across(d):
+        spread(d).wait_recv()
+        for e in range(1, half):
+            across(d, e).start()
+
+    def pass_to_core(d):
+        for e in range(1, half):
+            across(d, e).wait_recv()
+        to_core(d).start()
+
+    for d in range(1, groups):
+        spread(d).start()
+
     loads[1].wait()
     place = lax.broadcasted_iota(jnp.int32, (passage_slots, width), 0)
 
@@ -70,21 +113,6 @@
         return carry
 
     lax.fori_loop(0, pass_local, fill, 0)
-    table[...] = jnp.zeros_like(table)
-    pl.semaphore_wait(barrier, owners - 1)
-
-    def piece(g, owner):
-        at = lax.rem(owner, 2) * half + owner // 2
-        return tokens.at[g, pl.ds(pl.multiple_of(at * rows, rows), rows), :]
-
-    first = []
-    for d in range(1, groups):
-        copy = pltpu.make_async_remote_copy(
-            src_ref=piece(f, p), dst_ref=piece(f, p), send_sem=send_a.at[d], recv_sem=recv_a.at[d],
-            device_id=axis_pair(lax.rem(f + d, groups), p), device_id_type=MESH,
-        )
-        copy.start()
-        first.append(copy)
 
     columns = query_local * slots
     chosen = (
@@ -92,21 +120,19 @@
         == lax.broadcasted_iota(jnp.int32, (query_local, columns), 1) // slots
     ).astype(jnp.float32)
 
-    def score(g, d):
-        def step(i, carry):
-            passages = packed[pl.ds(i * block, block)].reshape(block * passage_slots, width)
-            for s in range(0, columns, part_tile):
-                similarity = lax.dot_general(
-                    passages,
-                    tokens[g, s : s + part_tile, :],
-                    (((1,), (1,)), ((), ())),
-                    preferred_element_type=jnp.float32,
-                )
-                found = jnp.max(similarity.reshape(block, passage_slots // 8, 8, part_tile), axis=1)
-                best[i, :, s : s + part_tile] = jnp.max(found, axis=1)
-            return carry
-
-        lax.fori_loop(0, pass_local // block, step, 0)
+    def score_block(g, i):
+        passages = packed[pl.ds(i * block, block)].reshape(block * passage_slots, width)
+        for s in range(0, columns, part_tile):
+            similarity = lax.dot_general(
+                passages,
+                tokens[g, s : s + part_tile, :],
+                (((1,), (1,)), ((), ())),
+                preferred_element_type=jnp.float32,
+            )
+            found = jnp.max(similarity.reshape(block, passage_slots // 8, 8, part_tile), axis=1)
+            best[i, :, s : s + part_tile] = jnp.max(found, axis=1)
+
+    def total_up(d):
         summed = lax.dot_general(
             chosen,
             best[...].reshape(pass_local, columns),
@@ -132,22 +158,6 @@
             return carry
 
         lax.fori_loop(least, shards, go, 0)
-
-    score(f, 0)
-    out_ref[me] = table[0]
-    send_home(0, 1)
-
-    second = []
-    for d in range(1, groups):
-        first[d - 1].wait_recv()
-        g = lax.rem(f - d + groups, groups)
-        for e in range(1, half):
-            copy = pltpu.make_async_remote_copy(
-                src_ref=piece(g, p), dst_ref=piece(g, p), send_sem=send_b.at[d, e], recv_sem=recv_b.at[d, e],
-                device_id=axis_pair(f, lax.rem(p + 2 * e, shards)), device_id_type=MESH,
-            )
-            copy.start()
-            second.append(copy)
 
     loads[2].wait()
     loads[3].wait()
@@ -159,18 +169,18 @@
             preferred_element_type=jnp.float32,
         )
 
-    third = []
-    for d in range(1, groups):
-        g = lax.rem(f - d + groups, groups)
-        for e in range(1, half):
-            second[(d - 1) * (half - 1) + e - 1].wait_recv()
-        mine = tokens.at[g, pl.ds(pl.multiple_of(core * (half * rows), half * rows), half * rows), :]
-        copy = pltpu.make_async_remote_copy(
-            src_ref=mine, dst_ref=mine, send_sem=send_c.at[d], recv_sem=recv_c.at[d],
-            device_id=axis_pair(f, other), device_id_type=MESH,
-        )
-        copy.start()
-        third.append(copy)
+    blocks = pass_local // block
+    for d in range(1, min(3, groups)):
+        pass_across(d)
+    for i in range(blocks - 1):
+        score_block(f, i)
+    for d in range(3, min(4, groups)):
+        pass_across(d)
+    pass_to_core(1)
+    score_block(f, blocks - 1)
+    total_up(0)
+    out_ref[me] = table[0]
+    send_home(0, 1)
 
     sums = []
     for d in range(1, groups):
@@ -184,12 +194,19 @@
 
     def one_group(d, carry):
         g = lax.rem(f - d + groups, groups)
-        mine = tokens.at[g, pl.ds(pl.multiple_of(core * (half * rows), half * rows), half * rows), :]
-        pltpu.make_async_remote_copy(
-            src_ref=mine, dst_ref=mine, send_sem=send_c.at[d], recv_sem=recv_c.at[d],
-            device_id=axis_pair(f, other), device_id_type=MESH,
-        ).wait_recv()
-        score(g, d)
+
+        @pl.when(d + 3 < groups)
+        def _():
+            pass_across(d + 3)
+
+        @pl.when(d + 1 < groups)
+        def _():
+            pass_to_core(d + 1)
+
+        to_core(d).wait_recv()
+        for i in range(blocks):
+            score_block(g, i)
+        total_up(d)
         send_home(d, 0)
         return carry
 
@@ -200,8 +217,13 @@
         sums[d - 1].wait_recv()
         total = total + landed[d]
     fde_ref[...] = total
-    for copy in first + second + third + sums:
+    for copy in sums:
         copy.wait_send()
+    for d in range(1, groups):
+        spread(d).wait_send()
+        for e in range(1, half):
+            across(d, e).wait_send()
+        to_core(d).wait_send()
 
     def finish(at, carry):
         home(at // shards, lax.rem(at, shards)).wait()
@@ -248,7 +270,7 @@
             dma((owners,)), dma((owners,)),
         ],
         compiler_params=pltpu.CompilerParams(
-            collective_id=0, has_side_effects=True, vmem_limit_bytes=40 * 1024 * 1024
+            collective_id=0, has_side_effects=True, vmem_limit_bytes=60 * 1024 * 1024
         ),
         name="retrieve",
     )(totals, lengths, qfe, pfde, query_tokens, passage_tokens)

time: 54.4 us -> 44.4 us (0.82)
  Pallas kernels: 45.4 us -> 39.7 us
  local copies, waits for them, and re-layouts: 6.89 us -> 2.65 us
    pallas_call x1, Pallas kernels: 45.4 us -> 39.7 us  [call(): pl.pallas_call(functools.partial(kernel, groups, shards), out_shape=(jax....]
    unnamed x17 -> x5, local copies, waits for them, and re-layouts: 6.47 us -> 1.33 us
    reshape x2, local copies, waits for them, and re-layouts: 0.28 us -> 1.18 us  [body(): back[:, :, :packs * pass_local]]
where the time goes in v4:
time: 44.4 us; the launch traced here: 44.1 us
  Pallas kernels  39.7 us (89%)
  local copies, waits for them, and re-layouts  2.65 us (6%)
  other arithmetic  1.09 us (2%)
  between operations  0.69 us (2%)
    pallas_call x1, Pallas kernels, call(): pl.pallas_call(functools.partial(kernel, groups, shards), out_shape=(jax....  39.7 us
    unnamed x5, local copies, waits for them, and re-layouts  1.33 us
    reshape x2, local copies, waits for them, and re-layouts, body(): back[:, :, :packs * pass_local]  1.18 us

profile of v4, /device:TPU:0, one launch (start us, length us, event | category | flops | bytes accessed | tf_op | source)
XLA Modules:
  0.0 44.1 jit_solution(4193914371650553544)
XLA Ops:
  0.6 0.0 copy-start.1
  0.6 0.0 copy-start
  0.7 39.7 %retrieve.1 = (f32[32,8,128]{2,1,0:T(8,128)}, f32[16,256]{1,0:T(8,128)}) custom-call(s32[16]{0:T(128)} %totals_ref.1, s32[32]{0:T(128)} %len_ref.1, bf16[128,1280]{1,0:T(8,128)(2,1)} %qfe_hbm.1, bf16[256,1280]{1,0:T(8,128)(2,1)} %pfde_hbm.1, bf16[16,32,128]{2,1,0:T(8,128)(2,1)} %tok_hbm.1, bf16[32,256,128]{2,1,0:T(8,128)(2,1)} %pass_hbm.1), custom_call_target="tpu_custom_call" | custom-call | tf_op jit(solution)/shard_map/retrieve/pallas_call | solution.py:247
  40.4 1.1 %reshape.10 = f32[32,8,2,32]{3,2,1,0:T(2,128)S(1)} reshape(f32[32,8,64]{2,1,0:T(8,128)} %bitcast.7) | data formatting | bytes 131072 | tf_op jit(solution)/shard_map/reshape | solution.py:298
  41.5 0.1 copy.12
  41.5 0.1 broadcast_in_dim.17
  41.7 0.0 copy-done
  41.7 0.4 select_reduce_fusion
  42.1 0.0 copy-done.1
  42.1 0.7 %broadcast_divide_fusion = f32[16,32]{1,0:T(8,128)} fusion(f32[16,32]{1,0:T(8,128)S(1)} %select_reduce_fusion, f32[16]{0:T(128)S(1)} %convert_element_type.3), kind=kLoop, calls=%fused_computation.3 | loop fusion | flops 512 | bytes 4160 | tf_op jit(solution)/shard_map/div | solution.py:304
  42.8 1.3 %copy.14 = f32[16,256]{1,0:T(8,128)} copy(f32[16,256]{1,0:T(8,128)} %get-tuple-element.8) | data formatting | bytes 32768
  (1 shorter events, 0.0 us)
Async XLA Ops:
  0.6 41.5 %copy-start.1 = (s32[16]{0:T(128)S(1)}, s32[16]{0:T(128)}, u32[]{:S(2)}) copy-start(s32[16]{0:T(128)} %totals_ref.1) | copy-start | bytes 196
  0.6 41.0 %copy-start = (s32[16,32]{1,0:T(8,128)S(1)}, s32[16,32]{1,0:T(8,128)}, u32[]{:S(2)}) copy-start(s32[16,32]{1,0:T(8,128)} %param.13) | copy-start | bytes 6148
